TPU v7x, 256 devices: a whole 4x4x8 slice. The times are simulated.
256 devices in a mesh: leaf: 256 (over z, y, x, core).
Axes of the slice: x: 4, y: 4, z: 8, core: 2. Of those that a mesh axis runs over, the one named last changes fastest.
Arguments:
- loads: bfloat16 [524288, 128], P('leaf'), may hold values from -6 to 6
- leaf_inverse: bfloat16 [524288, 2048], P('leaf'), may hold values from -0.125 to 0.125
- bases: bfloat16 [5, 524288, 128], P(None, 'leaf'), may hold values from -0.375 to 0.375
- couplings: bfloat16 [5, 256, 256, 256], P(None, 'leaf'), as said below
Outputs:
- solution: float32 [524288, 128], P('leaf')
Inputs may be any that keep to these rules, and one draw needn't show every extreme that they name: couplings[l, d] is the same matrix for all leaves d of one level-l node, that is for each run of 256 / 2**l consecutive leaves.
All inputs are finite; a program needn't handle non-finite values.
Results may differ from a plain program's by a relative error of at most 0.018.
Values sent between devices are 32-bit elements; how exact they have to be, the bound alone decides.
A program may use at most 64 MiB of HBM per device.

v0:
```python
import jax
import jax.numpy as jnp
from jax import lax
from jax.sharding import PartitionSpec as P


def from_partner(value, axis, stride):
    mask = 2**stride
    pairs = [(source, source ^ mask) for source in range(lax.axis_size(axis))]
    return lax.ppermute(value, axis, pairs)


def pair_total(own_terms, span_bits, child_side):
    child_total = own_terms
    for bit_no in range(span_bits - 1):
        child_total = child_total + from_partner(child_total, "leaf", bit_no)
    sibling = from_partner(child_total, "leaf", span_bits - 1)
    return jnp.where(
        child_side == 0,
        jnp.concatenate([child_total, sibling], 0),
        jnp.concatenate([sibling, child_total], 0),
    )


def sweep(field, bases, couplings, own_index, tree_depth):
    levels = bases.shape[0]
    rank = bases.shape[2]
    for sweep_turn in range(levels):
        level_no = levels - 1 - sweep_turn
        span_bits = tree_depth - level_no
        child_side = own_index >> span_bits - 1 & 1
        field_b = field.astype(jnp.bfloat16)
        own_terms = jnp.einsum(
            "nr,nk->rk", bases[level_no], field_b, preferred_element_type=jnp.float32
        )
        group_total = pair_total(own_terms, span_bits, child_side)
        node_cap = couplings[level_no, 0].astype(jnp.float32)
        coeffs = jnp.dot(
            node_cap,
            group_total,
            precision=lax.Precision.HIGHEST,
            preferred_element_type=jnp.float32,
        ).astype(jnp.bfloat16)
        own_coeffs = lax.dynamic_slice_in_dim(coeffs, child_side * rank, rank, 0)
        field = field - jnp.dot(bases[level_no], own_coeffs, preferred_element_type=jnp.float32)
    return field


def local(loads, leaf_inverse, bases, couplings):
    leaves = lax.axis_size("leaf")
    tree_depth = leaves.bit_length() - 1
    own_index = lax.axis_index("leaf")
    field = jnp.dot(leaf_inverse, loads, preferred_element_type=jnp.float32)
    return sweep(field, bases, couplings, own_index, tree_depth)


def solution(mesh):
    in_specs = (
        P("leaf", None),
        P("leaf", None),
        P(None, "leaf", None),
        P(None, "leaf", None, None),
    )
    out_specs = P("leaf", None)
    return jax.shard_map(local, mesh=mesh, in_specs=in_specs, out_specs=out_specs, check_vma=False)
```

profile of v0, /device:TPU:18, one launch (start us, length us, event | category | flops | bytes accessed | tf_op | source)
XLA Modules:
  0.0 167.9 jit_solution(3262443297432950197)
XLA Ops:
  1.0 5.8 %fusion.85 = f32[2048,128]{1,0:T(8,128)S(1)} fusion(bf16[2048,2048]{1,0:T(8,128)(2,1)} %param.5, bf16[2048,128]{1,0:T(8,128)(2,1)S(1)} %copy-done), kind=kOutput, calls=%fused_computation.105 | convolution fusion | flops 1073741824 | bytes 9961472 | tf_op jit(solution)/shard_map/dot_general | solution.py:53
  10.1 3.7 %collective-permute-done.1 = f32[128,128]{1,0:T(8,128)S(1)} collective-permute-done((f32[128,128]{1,0:T(8,128)S(1)}, f32[128,128]{1,0:T(8,128)S(1)}, u32[]{:S(2)}, u32[]{:S(2)}) %collective-permute-start.1) | collective-permute-done | bytes 65568 | tf_op jit(solution)/shard_map/ppermute | solution.py:10
  16.1 3.6 %collective-permute-done.2 = f32[128,128]{1,0:T(8,128)S(1)} collective-permute-done((f32[128,128]{1,0:T(8,128)S(1)}, f32[128,128]{1,0:T(8,128)S(1)}, u32[]{:S(2)}, u32[]{:S(2)}) %collective-permute-start.2) | collective-permute-done | bytes 65568 | tf_op jit(solution)/shard_map/ppermute | solution.py:10
  21.1 3.0 %collective-permute-done.3 = f32[128,128]{1,0:T(8,128)S(1)} collective-permute-done((f32[128,128]{1,0:T(8,128)S(1)}, f32[128,128]{1,0:T(8,128)S(1)}, u32[]{:S(2)}, u32[]{:S(2)}) %collective-permute-start.3) | collective-permute-done | bytes 65568 | tf_op jit(solution)/shard_map/ppermute | solution.py:10
  30.1 3.7 %collective-permute-done.5 = f32[128,128]{1,0:T(8,128)S(1)} collective-permute-done((f32[128,128]{1,0:T(8,128)S(1)}, f32[128,128]{1,0:T(8,128)S(1)}, u32[]{:S(2)}, u32[]{:S(2)}) %collective-permute-start.5) | collective-permute-done | bytes 65568 | tf_op jit(solution)/shard_map/ppermute | solution.py:10
  36.1 3.6 %collective-permute-done.6 = f32[128,128]{1,0:T(8,128)S(1)} collective-permute-done((f32[128,128]{1,0:T(8,128)S(1)}, f32[128,128]{1,0:T(8,128)S(1)}, u32[]{:S(2)}, u32[]{:S(2)}) %collective-permute-start.6) | collective-permute-done | bytes 65568 | tf_op jit(solution)/shard_map/ppermute | solution.py:10
  41.1 3.1 %collective-permute-done.7 = f32[128,128]{1,0:T(8,128)S(1)} collective-permute-done((f32[128,128]{1,0:T(8,128)S(1)}, f32[128,128]{1,0:T(8,128)S(1)}, u32[]{:S(2)}, u32[]{:S(2)}) %collective-permute-start.7) | collective-permute-done | bytes 65568 | tf_op jit(solution)/shard_map/ppermute | solution.py:10
  45.0 5.1 %collective-permute-done.8 = f32[128,128]{1,0:T(8,128)S(1)} collective-permute-done((f32[128,128]{1,0:T(8,128)S(1)}, f32[128,128]{1,0:T(8,128)S(1)}, u32[]{:S(2)}, u32[]{:S(2)}) %collective-permute-start.8) | collective-permute-done | bytes 65568 | tf_op jit(solution)/shard_map/ppermute | solution.py:10
  56.0 3.9 %collective-permute-done.10 = f32[128,128]{1,0:T(8,128)S(1)} collective-permute-done((f32[128,128]{1,0:T(8,128)S(1)}, f32[128,128]{1,0:T(8,128)S(1)}, u32[]{:S(2)}, u32[]{:S(2)}) %collective-permute-start.10) | collective-permute-done | bytes 65568 | tf_op jit(solution)/shard_map/ppermute | solution.py:10
  59.9 2.3 %collective-permute-start.11 = (f32[128,128]{1,0:T(8,128)S(1)}, f32[128,128]{1,0:T(8,128)S(1)}, u32[]{:S(2)}, u32[]{:S(2)}) collective-permute-start(f32[128,128]{1,0:T(8,128)S(1)} %add.100), channel_id=1, source_target_pairs={{0,4},{1,5},{2,6},{3,7},{4,0},{5,1},{6,2},{7,3},{8,12},{9,13},{10,... | collective-permute-start | bytes 196616 | tf_op jit(solution)/shard_map/ppermute | solution.py:10
  62.1 3.6 %collective-permute-done.11 = f32[128,128]{1,0:T(8,128)S(1)} collective-permute-done((f32[128,128]{1,0:T(8,128)S(1)}, f32[128,128]{1,0:T(8,128)S(1)}, u32[]{:S(2)}, u32[]{:S(2)}) %collective-permute-start.11) | collective-permute-done | bytes 65568 | tf_op jit(solution)/shard_map/ppermute | solution.py:10
  67.4 2.7 %collective-permute-done.12 = f32[128,128]{1,0:T(8,128)S(1)} collective-permute-done((f32[128,128]{1,0:T(8,128)S(1)}, f32[128,128]{1,0:T(8,128)S(1)}, u32[]{:S(2)}, u32[]{:S(2)}) %collective-permute-start.12) | collective-permute-done | bytes 65568 | tf_op jit(solution)/shard_map/ppermute | solution.py:10
  71.4 4.6 %collective-permute-done.13 = f32[128,128]{1,0:T(8,128)S(1)} collective-permute-done((f32[128,128]{1,0:T(8,128)S(1)}, f32[128,128]{1,0:T(8,128)S(1)}, u32[]{:S(2)}, u32[]{:S(2)}) %collective-permute-start.13) | collective-permute-done | bytes 65568 | tf_op jit(solution)/shard_map/ppermute | solution.py:10
  76.0 2.6 %collective-permute-start.14 = (f32[128,128]{1,0:T(8,128)S(1)}, f32[128,128]{1,0:T(8,128)S(1)}, u32[]{:S(2)}, u32[]{:S(2)}) collective-permute-start(f32[128,128]{1,0:T(8,128)S(1)} %add.103), channel_id=1, source_target_pairs={{0,32},{1,33},{2,34},{3,35},{4,36},{5,37},{6,38},{7,39},{8,40},{9,... | collective-permute-start | bytes 196616 | tf_op jit(solution)/shard_map/ppermute | solution.py:10
  78.6 2.2 %collective-permute-done.14 = f32[128,128]{1,0:T(8,128)S(1)} collective-permute-done((f32[128,128]{1,0:T(8,128)S(1)}, f32[128,128]{1,0:T(8,128)S(1)}, u32[]{:S(2)}, u32[]{:S(2)}) %collective-permute-start.14) | collective-permute-done | bytes 65568 | tf_op jit(solution)/shard_map/ppermute | solution.py:10
  86.9 3.7 %collective-permute-done.16 = f32[128,128]{1,0:T(8,128)S(1)} collective-permute-done((f32[128,128]{1,0:T(8,128)S(1)}, f32[128,128]{1,0:T(8,128)S(1)}, u32[]{:S(2)}, u32[]{:S(2)}) %collective-permute-start.16) | collective-permute-done | bytes 65568 | tf_op jit(solution)/shard_map/ppermute | solution.py:10
  90.6 2.3 %collective-permute-start.17 = (f32[128,128]{1,0:T(8,128)S(1)}, f32[128,128]{1,0:T(8,128)S(1)}, u32[]{:S(2)}, u32[]{:S(2)}) collective-permute-start(f32[128,128]{1,0:T(8,128)S(1)} %add.106), channel_id=1, source_target_pairs={{0,4},{1,5},{2,6},{3,7},{4,0},{5,1},{6,2},{7,3},{8,12},{9,13},{10,... | collective-permute-start | bytes 196616 | tf_op jit(solution)/shard_map/ppermute | solution.py:10
  92.9 3.6 %collective-permute-done.17 = f32[128,128]{1,0:T(8,128)S(1)} collective-permute-done((f32[128,128]{1,0:T(8,128)S(1)}, f32[128,128]{1,0:T(8,128)S(1)}, u32[]{:S(2)}, u32[]{:S(2)}) %collective-permute-start.17) | collective-permute-done | bytes 65568 | tf_op jit(solution)/shard_map/ppermute | solution.py:10
  98.2 2.6 %collective-permute-done.18 = f32[128,128]{1,0:T(8,128)S(1)} collective-permute-done((f32[128,128]{1,0:T(8,128)S(1)}, f32[128,128]{1,0:T(8,128)S(1)}, u32[]{:S(2)}, u32[]{:S(2)}) %collective-permute-start.18) | collective-permute-done | bytes 65568 | tf_op jit(solution)/shard_map/ppermute | solution.py:10
  102.2 4.5 %collective-permute-done.19 = f32[128,128]{1,0:T(8,128)S(1)} collective-permute-done((f32[128,128]{1,0:T(8,128)S(1)}, f32[128,128]{1,0:T(8,128)S(1)}, u32[]{:S(2)}, u32[]{:S(2)}) %collective-permute-start.19) | collective-permute-done | bytes 65568 | tf_op jit(solution)/shard_map/ppermute | solution.py:10
  106.7 2.8 %collective-permute-start.20 = (f32[128,128]{1,0:T(8,128)S(1)}, f32[128,128]{1,0:T(8,128)S(1)}, u32[]{:S(2)}, u32[]{:S(2)}) collective-permute-start(f32[128,128]{1,0:T(8,128)S(1)} %add.109), channel_id=1, source_target_pairs={{0,32},{1,33},{2,34},{3,35},{4,36},{5,37},{6,38},{7,39},{8,40},{9,... | collective-permute-start | bytes 196616 | tf_op jit(solution)/shard_map/ppermute | solution.py:10
  109.5 2.2 %collective-permute-done.20 = f32[128,128]{1,0:T(8,128)S(1)} collective-permute-done((f32[128,128]{1,0:T(8,128)S(1)}, f32[128,128]{1,0:T(8,128)S(1)}, u32[]{:S(2)}, u32[]{:S(2)}) %collective-permute-start.20) | collective-permute-done | bytes 65568 | tf_op jit(solution)/shard_map/ppermute | solution.py:10
  111.8 3.4 %collective-permute-start.21 = (f32[128,128]{1,0:T(8,128)S(1)}, f32[128,128]{1,0:T(8,128)S(1)}, u32[]{:S(2)}, u32[]{:S(2)}) collective-permute-start(f32[128,128]{1,0:T(8,128)S(1)} %add.110), channel_id=1, source_target_pairs={{0,64},{1,65},{2,66},{3,67},{4,68},{5,69},{6,70},{7,71},{8,72},{9,... | collective-permute-start | bytes 196616 | tf_op jit(solution)/shard_map/ppermute | solution.py:10
  123.4 3.8 %collective-permute-done.23 = f32[128,128]{1,0:T(8,128)S(1)} collective-permute-done((f32[128,128]{1,0:T(8,128)S(1)}, f32[128,128]{1,0:T(8,128)S(1)}, u32[]{:S(2)}, u32[]{:S(2)}) %collective-permute-start.23) | collective-permute-done | bytes 65568 | tf_op jit(solution)/shard_map/ppermute | solution.py:10
  127.2 2.3 %collective-permute-start.24 = (f32[128,128]{1,0:T(8,128)S(1)}, f32[128,128]{1,0:T(8,128)S(1)}, u32[]{:S(2)}, u32[]{:S(2)}) collective-permute-start(f32[128,128]{1,0:T(8,128)S(1)} %add.113), channel_id=1, source_target_pairs={{0,4},{1,5},{2,6},{3,7},{4,0},{5,1},{6,2},{7,3},{8,12},{9,13},{10,... | collective-permute-start | bytes 196616 | tf_op jit(solution)/shard_map/ppermute | solution.py:10
  129.5 3.6 %collective-permute-done.24 = f32[128,128]{1,0:T(8,128)S(1)} collective-permute-done((f32[128,128]{1,0:T(8,128)S(1)}, f32[128,128]{1,0:T(8,128)S(1)}, u32[]{:S(2)}, u32[]{:S(2)}) %collective-permute-start.24) | collective-permute-done | bytes 65568 | tf_op jit(solution)/shard_map/ppermute | solution.py:10
  134.1 3.8 %collective-permute-done.25 = f32[128,128]{1,0:T(8,128)S(1)} collective-permute-done((f32[128,128]{1,0:T(8,128)S(1)}, f32[128,128]{1,0:T(8,128)S(1)}, u32[]{:S(2)}, u32[]{:S(2)}) %collective-permute-start.25) | collective-permute-done | bytes 65568 | tf_op jit(solution)/shard_map/ppermute | solution.py:10
  138.4 5.3 %collective-permute-done.26 = f32[128,128]{1,0:T(8,128)S(1)} collective-permute-done((f32[128,128]{1,0:T(8,128)S(1)}, f32[128,128]{1,0:T(8,128)S(1)}, u32[]{:S(2)}, u32[]{:S(2)}) %collective-permute-start.26) | collective-permute-done | bytes 65568 | tf_op jit(solution)/shard_map/ppermute | solution.py:10
  148.2 3.0 %collective-permute-start.28 = (f32[128,128]{1,0:T(8,128)S(1)}, f32[128,128]{1,0:T(8,128)S(1)}, u32[]{:S(2)}, u32[]{:S(2)}) collective-permute-start(f32[128,128]{1,0:T(8,128)S(1)} %add.117), channel_id=1, source_target_pairs={{0,64},{1,65},{2,66},{3,67},{4,68},{5,69},{6,70},{7,71},{8,72},{9,... | collective-permute-start | bytes 196616 | tf_op jit(solution)/shard_map/ppermute | solution.py:10
  151.2 2.2 %collective-permute-done.28 = f32[128,128]{1,0:T(8,128)S(1)} collective-permute-done((f32[128,128]{1,0:T(8,128)S(1)}, f32[128,128]{1,0:T(8,128)S(1)}, u32[]{:S(2)}, u32[]{:S(2)}) %collective-permute-start.28) | collective-permute-done | bytes 65568 | tf_op jit(solution)/shard_map/ppermute | solution.py:10
  153.5 8.5 %collective-permute-start.29 = (f32[128,128]{1,0:T(8,128)S(1)}, f32[128,128]{1,0:T(8,128)S(1)}, u32[]{:S(2)}, u32[]{:S(2)}) collective-permute-start(f32[128,128]{1,0:T(8,128)S(1)} %add.118), channel_id=1, source_target_pairs={{0,128},{1,129},{2,130},{3,131},{4,132},{5,133},{6,134},{7,135},{8... | collective-permute-start | bytes 196616 | tf_op jit(solution)/shard_map/ppermute | solution.py:10
  165.4 2.5 %fusion = f32[2048,128]{1,0:T(8,128)} fusion(f32[2048,128]{1,0:T(8,128)} %copy-done.2, bf16[5,2048,128]{2,1,0:T(8,128)(2,1)S(1)} %copy-done.1, bf16[128,256]{1,0:T(8,128)(2,1)S(1)} %fusion.54, s32[]{:T(128)S(6)} %select_n.61), kind=kOutput, calls=%fused_computation.1 | convolution fusion | flops 67371008 | bytes 2654212 | tf_op jit(solution)/shard_map/dot_general | solution.py:45
  (83 shorter events, 54.0 us)
Async XLA Ops:
  0.0 1.0 copy-start
  0.0 7.8 %copy-start.1 = (bf16[5,2048,128]{2,1,0:T(8,128)(2,1)S(1)}, bf16[5,2048,128]{2,1,0:T(8,128)(2,1)}, u32[]{:S(2)}) copy-start(bf16[5,2048,128]{2,1,0:T(8,128)(2,1)} %param.6) | copy-start | bytes 7864324
  8.1 1.3 collective-permute-start
  9.5 4.4 %collective-permute-start.1 = (f32[128,128]{1,0:T(8,128)S(1)}, f32[128,128]{1,0:T(8,128)S(1)}, u32[]{:S(2)}, u32[]{:S(2)}) collective-permute-start(f32[128,128]{1,0:T(8,128)S(1)} %add.90), channel_id=1, source_target_pairs={{0,2},{1,3},{2,0},{3,1},{4,6},{5,7},{6,4},{7,5},{8,10},{9,11},{10,... | collective-permute-start | bytes 196616 | tf_op jit(solution)/shard_map/ppermute | solution.py:10
  13.9 5.9 %collective-permute-start.2 = (f32[128,128]{1,0:T(8,128)S(1)}, f32[128,128]{1,0:T(8,128)S(1)}, u32[]{:S(2)}, u32[]{:S(2)}) collective-permute-start(f32[128,128]{1,0:T(8,128)S(1)} %add.91), channel_id=1, source_target_pairs={{0,4},{1,5},{2,6},{3,7},{4,0},{5,1},{6,2},{7,3},{8,12},{9,13},{10,... | collective-permute-start | bytes 196616 | tf_op jit(solution)/shard_map/ppermute | solution.py:10
  19.7 4.4 %collective-permute-start.3 = (f32[128,128]{1,0:T(8,128)S(1)}, f32[128,128]{1,0:T(8,128)S(1)}, u32[]{:S(2)}, u32[]{:S(2)}) collective-permute-start(f32[128,128]{1,0:T(8,128)S(1)} %add.92), channel_id=1, source_target_pairs={{0,8},{1,9},{2,10},{3,11},{4,12},{5,13},{6,14},{7,15},{8,0},{9,1},... | collective-permute-start | bytes 196616 | tf_op jit(solution)/shard_map/ppermute | solution.py:10
  28.1 1.3 collective-permute-start.4
  29.5 4.4 %collective-permute-start.5 = (f32[128,128]{1,0:T(8,128)S(1)}, f32[128,128]{1,0:T(8,128)S(1)}, u32[]{:S(2)}, u32[]{:S(2)}) collective-permute-start(f32[128,128]{1,0:T(8,128)S(1)} %add.94), channel_id=1, source_target_pairs={{0,2},{1,3},{2,0},{3,1},{4,6},{5,7},{6,4},{7,5},{8,10},{9,11},{10,... | collective-permute-start | bytes 196616 | tf_op jit(solution)/shard_map/ppermute | solution.py:10
  33.9 5.9 %collective-permute-start.6 = (f32[128,128]{1,0:T(8,128)S(1)}, f32[128,128]{1,0:T(8,128)S(1)}, u32[]{:S(2)}, u32[]{:S(2)}) collective-permute-start(f32[128,128]{1,0:T(8,128)S(1)} %add.95), channel_id=1, source_target_pairs={{0,4},{1,5},{2,6},{3,7},{4,0},{5,1},{6,2},{7,3},{8,12},{9,13},{10,... | collective-permute-start | bytes 196616 | tf_op jit(solution)/shard_map/ppermute | solution.py:10
  39.7 4.5 %collective-permute-start.7 = (f32[128,128]{1,0:T(8,128)S(1)}, f32[128,128]{1,0:T(8,128)S(1)}, u32[]{:S(2)}, u32[]{:S(2)}) collective-permute-start(f32[128,128]{1,0:T(8,128)S(1)} %add.96), channel_id=1, source_target_pairs={{0,8},{1,9},{2,10},{3,11},{4,12},{5,13},{6,14},{7,15},{8,0},{9,1},... | collective-permute-start | bytes 196616 | tf_op jit(solution)/shard_map/ppermute | solution.py:10
  44.2 5.9 %collective-permute-start.8 = (f32[128,128]{1,0:T(8,128)S(1)}, f32[128,128]{1,0:T(8,128)S(1)}, u32[]{:S(2)}, u32[]{:S(2)}) collective-permute-start(f32[128,128]{1,0:T(8,128)S(1)} %add.97), channel_id=1, source_target_pairs={{0,16},{1,17},{2,18},{3,19},{4,20},{5,21},{6,22},{7,23},{8,24},{9,... | collective-permute-start | bytes 196616 | tf_op jit(solution)/shard_map/ppermute | solution.py:10
  54.1 1.3 collective-permute-start.9
  55.5 4.4 %collective-permute-start.10 = (f32[128,128]{1,0:T(8,128)S(1)}, f32[128,128]{1,0:T(8,128)S(1)}, u32[]{:S(2)}, u32[]{:S(2)}) collective-permute-start(f32[128,128]{1,0:T(8,128)S(1)} %add.99), channel_id=1, source_target_pairs={{0,2},{1,3},{2,0},{3,1},{4,6},{5,7},{6,4},{7,5},{8,10},{9,11},{10,... | collective-permute-start | bytes 196616 | tf_op jit(solution)/shard_map/ppermute | solution.py:10
  59.9 5.9 %collective-permute-start.11 = (f32[128,128]{1,0:T(8,128)S(1)}, f32[128,128]{1,0:T(8,128)S(1)}, u32[]{:S(2)}, u32[]{:S(2)}) collective-permute-start(f32[128,128]{1,0:T(8,128)S(1)} %add.100), channel_id=1, source_target_pairs={{0,4},{1,5},{2,6},{3,7},{4,0},{5,1},{6,2},{7,3},{8,12},{9,13},{10,... | collective-permute-start | bytes 196616 | tf_op jit(solution)/shard_map/ppermute | solution.py:10
  65.7 4.4 %collective-permute-start.12 = (f32[128,128]{1,0:T(8,128)S(1)}, f32[128,128]{1,0:T(8,128)S(1)}, u32[]{:S(2)}, u32[]{:S(2)}) collective-permute-start(f32[128,128]{1,0:T(8,128)S(1)} %add.101), channel_id=1, source_target_pairs={{0,8},{1,9},{2,10},{3,11},{4,12},{5,13},{6,14},{7,15},{8,0},{9,1},... | collective-permute-start | bytes 196616 | tf_op jit(solution)/shard_map/ppermute | solution.py:10
  70.1 5.9 %collective-permute-start.13 = (f32[128,128]{1,0:T(8,128)S(1)}, f32[128,128]{1,0:T(8,128)S(1)}, u32[]{:S(2)}, u32[]{:S(2)}) collective-permute-start(f32[128,128]{1,0:T(8,128)S(1)} %add.102), channel_id=1, source_target_pairs={{0,16},{1,17},{2,18},{3,19},{4,20},{5,21},{6,22},{7,23},{8,24},{9,... | collective-permute-start | bytes 196616 | tf_op jit(solution)/shard_map/ppermute | solution.py:10
  76.0 4.9 %collective-permute-start.14 = (f32[128,128]{1,0:T(8,128)S(1)}, f32[128,128]{1,0:T(8,128)S(1)}, u32[]{:S(2)}, u32[]{:S(2)}) collective-permute-start(f32[128,128]{1,0:T(8,128)S(1)} %add.103), channel_id=1, source_target_pairs={{0,32},{1,33},{2,34},{3,35},{4,36},{5,37},{6,38},{7,39},{8,40},{9,... | collective-permute-start | bytes 196616 | tf_op jit(solution)/shard_map/ppermute | solution.py:10
  84.9 1.3 collective-permute-start.15
  86.3 4.4 %collective-permute-start.16 = (f32[128,128]{1,0:T(8,128)S(1)}, f32[128,128]{1,0:T(8,128)S(1)}, u32[]{:S(2)}, u32[]{:S(2)}) collective-permute-start(f32[128,128]{1,0:T(8,128)S(1)} %add.105), channel_id=1, source_target_pairs={{0,2},{1,3},{2,0},{3,1},{4,6},{5,7},{6,4},{7,5},{8,10},{9,11},{10,... | collective-permute-start | bytes 196616 | tf_op jit(solution)/shard_map/ppermute | solution.py:10
  90.6 5.9 %collective-permute-start.17 = (f32[128,128]{1,0:T(8,128)S(1)}, f32[128,128]{1,0:T(8,128)S(1)}, u32[]{:S(2)}, u32[]{:S(2)}) collective-permute-start(f32[128,128]{1,0:T(8,128)S(1)} %add.106), channel_id=1, source_target_pairs={{0,4},{1,5},{2,6},{3,7},{4,0},{5,1},{6,2},{7,3},{8,12},{9,13},{10,... | collective-permute-start | bytes 196616 | tf_op jit(solution)/shard_map/ppermute | solution.py:10
  96.5 4.4 %collective-permute-start.18 = (f32[128,128]{1,0:T(8,128)S(1)}, f32[128,128]{1,0:T(8,128)S(1)}, u32[]{:S(2)}, u32[]{:S(2)}) collective-permute-start(f32[128,128]{1,0:T(8,128)S(1)} %add.107), channel_id=1, source_target_pairs={{0,8},{1,9},{2,10},{3,11},{4,12},{5,13},{6,14},{7,15},{8,0},{9,1},... | collective-permute-start | bytes 196616 | tf_op jit(solution)/shard_map/ppermute | solution.py:10
  100.9 5.9 %collective-permute-start.19 = (f32[128,128]{1,0:T(8,128)S(1)}, f32[128,128]{1,0:T(8,128)S(1)}, u32[]{:S(2)}, u32[]{:S(2)}) collective-permute-start(f32[128,128]{1,0:T(8,128)S(1)} %add.108), channel_id=1, source_target_pairs={{0,16},{1,17},{2,18},{3,19},{4,20},{5,21},{6,22},{7,23},{8,24},{9,... | collective-permute-start | bytes 196616 | tf_op jit(solution)/shard_map/ppermute | solution.py:10
  106.7 5.0 %collective-permute-start.20 = (f32[128,128]{1,0:T(8,128)S(1)}, f32[128,128]{1,0:T(8,128)S(1)}, u32[]{:S(2)}, u32[]{:S(2)}) collective-permute-start(f32[128,128]{1,0:T(8,128)S(1)} %add.109), channel_id=1, source_target_pairs={{0,32},{1,33},{2,34},{3,35},{4,36},{5,37},{6,38},{7,39},{8,40},{9,... | collective-permute-start | bytes 196616 | tf_op jit(solution)/shard_map/ppermute | solution.py:10
  111.8 5.7 %collective-permute-start.21 = (f32[128,128]{1,0:T(8,128)S(1)}, f32[128,128]{1,0:T(8,128)S(1)}, u32[]{:S(2)}, u32[]{:S(2)}) collective-permute-start(f32[128,128]{1,0:T(8,128)S(1)} %add.110), channel_id=1, source_target_pairs={{0,64},{1,65},{2,66},{3,67},{4,68},{5,69},{6,70},{7,71},{8,72},{9,... | collective-permute-start | bytes 196616 | tf_op jit(solution)/shard_map/ppermute | solution.py:10
  121.5 1.3 collective-permute-start.22
  122.8 4.4 %collective-permute-start.23 = (f32[128,128]{1,0:T(8,128)S(1)}, f32[128,128]{1,0:T(8,128)S(1)}, u32[]{:S(2)}, u32[]{:S(2)}) collective-permute-start(f32[128,128]{1,0:T(8,128)S(1)} %add.112), channel_id=1, source_target_pairs={{0,2},{1,3},{2,0},{3,1},{4,6},{5,7},{6,4},{7,5},{8,10},{9,11},{10,... | collective-permute-start | bytes 196616 | tf_op jit(solution)/shard_map/ppermute | solution.py:10
  127.2 5.9 %collective-permute-start.24 = (f32[128,128]{1,0:T(8,128)S(1)}, f32[128,128]{1,0:T(8,128)S(1)}, u32[]{:S(2)}, u32[]{:S(2)}) collective-permute-start(f32[128,128]{1,0:T(8,128)S(1)} %add.113), channel_id=1, source_target_pairs={{0,4},{1,5},{2,6},{3,7},{4,0},{5,1},{6,2},{7,3},{8,12},{9,13},{10,... | collective-permute-start | bytes 196616 | tf_op jit(solution)/shard_map/ppermute | solution.py:10
  133.1 4.8 %collective-permute-start.25 = (f32[128,128]{1,0:T(8,128)S(1)}, f32[128,128]{1,0:T(8,128)S(1)}, u32[]{:S(2)}, u32[]{:S(2)}) collective-permute-start(f32[128,128]{1,0:T(8,128)S(1)} %add.114), channel_id=1, source_target_pairs={{0,8},{1,9},{2,10},{3,11},{4,12},{5,13},{6,14},{7,15},{8,0},{9,1},... | collective-permute-start | bytes 196616 | tf_op jit(solution)/shard_map/ppermute | solution.py:10
  137.9 5.9 %collective-permute-start.26 = (f32[128,128]{1,0:T(8,128)S(1)}, f32[128,128]{1,0:T(8,128)S(1)}, u32[]{:S(2)}, u32[]{:S(2)}) collective-permute-start(f32[128,128]{1,0:T(8,128)S(1)} %add.115), channel_id=1, source_target_pairs={{0,16},{1,17},{2,18},{3,19},{4,20},{5,21},{6,22},{7,23},{8,24},{9,... | collective-permute-start | bytes 196616 | tf_op jit(solution)/shard_map/ppermute | solution.py:10
  143.8 4.5 %collective-permute-start.27 = (f32[128,128]{1,0:T(8,128)S(1)}, f32[128,128]{1,0:T(8,128)S(1)}, u32[]{:S(2)}, u32[]{:S(2)}) collective-permute-start(f32[128,128]{1,0:T(8,128)S(1)} %add.116), channel_id=1, source_target_pairs={{0,32},{1,33},{2,34},{3,35},{4,36},{5,37},{6,38},{7,39},{8,40},{9,... | collective-permute-start | bytes 196616 | tf_op jit(solution)/shard_map/ppermute | solution.py:10
  148.2 5.3 %collective-permute-start.28 = (f32[128,128]{1,0:T(8,128)S(1)}, f32[128,128]{1,0:T(8,128)S(1)}, u32[]{:S(2)}, u32[]{:S(2)}) collective-permute-start(f32[128,128]{1,0:T(8,128)S(1)} %add.117), channel_id=1, source_target_pairs={{0,64},{1,65},{2,66},{3,67},{4,68},{5,69},{6,70},{7,71},{8,72},{9,... | collective-permute-start | bytes 196616 | tf_op jit(solution)/shard_map/ppermute | solution.py:10
  153.5 10.7 %collective-permute-start.29 = (f32[128,128]{1,0:T(8,128)S(1)}, f32[128,128]{1,0:T(8,128)S(1)}, u32[]{:S(2)}, u32[]{:S(2)}) collective-permute-start(f32[128,128]{1,0:T(8,128)S(1)} %add.118), channel_id=1, source_target_pairs={{0,128},{1,129},{2,130},{3,131},{4,132},{5,133},{6,134},{7,135},{8... | collective-permute-start | bytes 196616 | tf_op jit(solution)/shard_map/ppermute | solution.py:10
  (5 other events, 4.9 us)
where the time goes:
time: 168 us
  waiting for transfers between devices  91.2 us (54%)
  starting transfers between devices  48.3 us (29%)
  matrix products  22.1 us (13%)
  local copies, waits for them, and re-layouts  5.87 us (3%)
    ppermute x30, waiting for transfers between devices, from_partner(): return lax.ppermute(value, axis, pairs)  91.2 us
    ppermute x30, starting transfers between devices, from_partner(): return lax.ppermute(value, axis, pairs)  48.3 us
    dot_general x5, matrix products, sweep(): jnp.dot(bases[level_no], own_coeffs, preferred_element_type=jnp.float32)  8.61 us
    dot_general x5, matrix products, sweep(): jnp.dot(node_cap, group_total, precision=lax.Precision.HIGHEST, preferred...  6.02 us
    unnamed x14, local copies, waits for them, and re-layouts  5.87 us
    dot_general x1, matrix products, local(): field = jnp.dot(leaf_inverse, loads, preferred_element_type=jnp.float32)  5.76 us
  transfers between devices with their start and end apart: 30, of which 30 were waited for; matrix products, arithmetic and copies ran while one was open for 0% of the time, Pallas kernels for 0%

commit v1 on v0

v1 whole, which is shorter than its diff:
```python
import jax
import jax.numpy as jnp
from jax import lax
from jax.experimental import pallas as pl
from jax.experimental.pallas import tpu as pltpu
from jax.sharding import PartitionSpec as P

MESH = pl.DeviceIdType.MESH
F32 = jnp.float32
BF16 = jnp.bfloat16
RANK = 128
CASES = 128
LEVELS = 5
QUARTER = CASES // 4
ROWS = 256


def flip(value, bit):
    return value + bit - 2 * bit * ((value // bit) % 2)


def flips(value, mask):
    for bit in (1, 2, 4):
        if mask & bit:
            value = flip(value, bit)
    return value


def dot_tn(a, b):
    return lax.dot_general(a, b, (((0,), (0,)), ((), ())), preferred_element_type=F32)


def dot_nt(a, b):
    return lax.dot_general(a, b, (((1,), (1,)), ((), ())), preferred_element_type=F32)


def two_parts(value):
    high = value.astype(BF16)
    return high, (value - high.astype(F32)).astype(BF16)


def times_gram(z, gram):
    high, low = two_parts(gram)
    return jnp.dot(
        jnp.concatenate([z, z], 1), jnp.concatenate([high, low], 0), preferred_element_type=F32
    )


GROUPS = (((4, 3),), ((4, 2), (3, 2)), ((4, 0), (4, 1), (3, 0), (3, 1)), ((2, 0), (2, 1), (1, 0)))


def tree_kernel(
    loads_hbm, inverse_hbm, bases_hbm, caps_hbm,
    part_hbm, z0_out,
    loads, inverse, bcat, caps, field, pacc,
    sa, sb, sc, sd, sa_in, sb_in, sc_in, sd_in, sa_rs, sb_rs, sc_rs, sd_rs,
    sa_own, sb_own, sc_own, sd_own, sd_y, gd_own, se_own, se_z, ge_own,
    ga, gb, gc, gd, ge,
    p4, p3, pr, p4_in, p3_in, pr_in, p4_rs, p3_rs, pr_rs,
    e3, l3, e2, l2, e10, l2r, e1, l1, f0, l1r, e0, l0,
    zown, zbuf,
    local_sem, chunk_sem, out_sem, send_sem, recv_sem,
):
    rows = field.shape[0]
    steps = rows // ROWS
    me = lax.axis_index("leaf")
    core = me % 2
    x = (me // 2) % 4
    y = (me // 8) % 4
    z = me // 32

    def device(dx=0, dy=0, dz=0, on=1):
        return ((flips(z, dz) * 4 + flips(y, dy)) * 4 + flips(x, dx)) * 2 + on

    loads_in = []
    for level in range(LEVELS):
        copy = pltpu.make_async_copy(
            bases_hbm.at[level], bcat.at[:, pl.ds(level * RANK, RANK)], local_sem.at[level]
        )
        copy.start()
        loads_in.append(copy)
    loads_copy = pltpu.make_async_copy(loads_hbm, loads, local_sem.at[LEVELS])
    loads_copy.start()
    caps_copy = pltpu.make_async_copy(caps_hbm, caps, local_sem.at[LEVELS + 1])

    def inverse_copy(step):
        part = pl.ds(pl.multiple_of(step * ROWS, ROWS), ROWS)
        return pltpu.make_async_copy(inverse_hbm.at[part], inverse.at[part], chunk_sem.at[step])

    for step in range(steps):
        inverse_copy(step).start()
    caps_copy.start()

    barrier = pltpu.get_barrier_semaphore()

    def greet(partners):
        for partner in partners:
            pl.semaphore_signal(barrier, inc=1, device_id=(partner,), device_id_type=MESH)

    gram_partners = (
        [device(dx=j, on=0) for j in (1, 2, 3)]
        + [device(dy=j, on=0) for j in (1, 2, 3)]
        + [device(dz=1, on=0)]
        + [device(dx=j, on=1) for j in range(4)]
    )
    chain_partners = (
        [device(dx=j, on=0) for j in range(4)]
        + [device(dx=j) for j in (1, 2, 3)]
        + [device(dx=j, dy=1) for j in range(4)]
        + [device(dy=j) for j in (2, 3)]
        + [device(dy=j, dz=1) for j in range(4)]
        + [device(dz=j) for j in (2, 3, 7, 5)]
    )

    @pl.when(core == 0)
    def _():
        greet(gram_partners)

    @pl.when(core == 1)
    def _():
        greet(chain_partners)

    for copy in loads_in:
        copy.wait()
    grams = (sa, sb, sc, sd)
    for ref in grams:
        ref[...] = jnp.zeros_like(ref)

    def gram_step(step, carry):
        part = pl.ds(pl.multiple_of(step * ROWS, ROWS), ROWS)
        for level in (4, 3, 2, 1):
            got = dot_tn(
                bcat[part, level * RANK : (level + 1) * RANK], bcat[part, : level * RANK]
            )
            for ref, group in zip(grams, GROUPS):
                for place, (source, target) in enumerate(group):
                    if source == level:
                        ref[:, place * RANK : (place + 1) * RANK] += got[
                            :, target * RANK : (target + 1) * RANK
                        ]
        return carry

    lax.fori_loop(0, steps, gram_step, 0)

    @pl.when(core == 0)
    def _():
        pl.semaphore_wait(barrier, len(gram_partners))

    @pl.when(core == 1)
    def _():
        pl.semaphore_wait(barrier, len(chain_partners))

    counter = [0]

    def message(src, dst, target):
        number = counter[0]
        counter[0] += 1
        return pltpu.make_async_remote_copy(
            src_ref=src, dst_ref=dst, send_sem=send_sem.at[number], recv_sem=recv_sem.at[number],
            device_id=(target,), device_id_type=MESH,
        )

    def quarter(index):
        return pl.ds(pl.multiple_of(index * QUARTER, QUARTER), QUARTER)

    other = device(on=1 - core)
    grams_in = (sa_in, sb_in, sc_in, sd_in)
    gram_pair = [message(src, dst, other) for src, dst in zip(grams, grams_in)]

    @pl.when(core == 1)
    def _():
        for copy in gram_pair:
            copy.start()

    loads_copy.wait()
    pacc[...] = jnp.zeros_like(pacc)

    def field_step(step, carry):
        inverse_copy(step).wait()
        part = pl.ds(pl.multiple_of(step * ROWS, ROWS), ROWS)
        got = jnp.dot(inverse[part, :], loads[...], preferred_element_type=F32)
        field[part, :] = got
        high, low = two_parts(got)
        pacc[...] += dot_tn(jnp.concatenate([high, low], 1), bcat[part, :])
        return carry

    lax.fori_loop(0, steps // 2, field_step, 0)

    rs_slots = (sa_rs, sb_rs, sc_rs, sd_rs)
    gram_rs = [
        [message(src.at[quarter(flips(x, j))], dst.at[j - 1], device(dx=j, on=0)) for j in (1, 2, 3)]
        for src, dst in zip(grams, rs_slots)
    ]

    def pair_sum(group):
        gram_pair[group].wait_recv()
        grams[group][...] += grams_in[group][...]
        for copy in gram_rs[group]:
            copy.start()

    @pl.when(core == 0)
    def _():
        for group in range(4):
            pair_sum(group)

    lax.fori_loop(steps // 2, steps, field_step, 0)

    ordered = (p4, p3, pr)
    columns = ((4 * RANK, 5 * RANK), (3 * RANK, 4 * RANK), (0, 3 * RANK))
    for ref, (low, high) in zip(ordered, columns):
        ref[...] = pacc[:CASES, low:high] + pacc[CASES:, low:high]

    ordered_in = (p4_in, p3_in, pr_in)
    proj_pair = [message(src, dst, other) for src, dst in zip(ordered, ordered_in)]
    own_q = quarter(x)

    z_targets = [(j, on) for on in (1, 0) for j in range(4) if (j, on) != (0, 1)]
    z_out = [
        [message(zown.at[level], zbuf.at[level, own_q], device(dx=j, on=on)) for j, on in z_targets]
        for level in range(LEVELS)
    ]

    def z_wait(level, on):
        for (j, to), copy in zip(z_targets, z_out[level]):
            if to == on:
                copy.wait_recv()

    def subtract(levels):
        factors = jnp.concatenate([zbuf[level].astype(BF16) for level in levels], 1)
        low, high = levels[0] * RANK, (levels[-1] + 1) * RANK

        def step_(step, carry):
            part = pl.ds(pl.multiple_of(step * ROWS, ROWS), ROWS)
            field[part, :] -= dot_nt(bcat[part, low:high], factors)
            return carry

        lax.fori_loop(0, steps, step_, 0)

    def finish(on):
        out = pltpu.make_async_copy(field, part_hbm, out_sem)
        out.start()
        z_wait(0, on)
        z0_out[...] = zbuf[0].astype(BF16)
        out.wait()

    caps_copy.wait()

    gram_own = (sa_own, sb_own, sc_own, sd_own)
    gram_out = [
        [message(src, dst.at[own_q], device(dx=j)) for j in range(4)]
        for src, dst in ((sa_own, ga), (sb_own, gb), (sc_own, gc), (gd_own, gd), (ge_own, ge))
    ]
    plane_out = [message(sd_own, sd_y.at[j - 1], device(dy=j, on=0)) for j in (1, 2, 3)]
    pair_out = message(se_own, se_z, device(dz=1, on=0))

    def row_sum(group):
        for copy in gram_rs[group]:
            copy.wait_recv()
        slots = rs_slots[group]
        gram_own[group][...] = (
            grams[group][own_q, :] + slots[0] + slots[1] + slots[2]
        )

    def start(copies):
        for copy in copies:
            copy.start()

    def wait_recv(copies):
        for copy in copies:
            copy.wait_recv()

    def wait_send(copies):
        for copy in copies:
            copy.wait_send()

    @pl.when(core == 0)
    def _():
        start(proj_pair)
        for group in (0, 1):
            row_sum(group)
            start(gram_out[group])
        row_sum(3)
        start(plane_out)
        row_sum(2)
        start(gram_out[2])
        wait_recv(plane_out)
        total = sd_own[...] + sd_y[0] + sd_y[1] + sd_y[2]
        gd_own[...] = total[:, : 2 * RANK]
        se_own[...] = total[:, 2 * RANK :]
        pair_out.start()
        start(gram_out[3])
        pair_out.wait_recv()
        ge_own[...] = se_own[...] + se_z[...]
        start(gram_out[4])
        for level in (4, 3, 2, 1):
            z_wait(level, 0)
        subtract((1, 2, 3, 4))
        finish(0)
        for copies in gram_rs + gram_out + [plane_out, [pair_out], proj_pair]:
            wait_send(copies)

    def child_side(level):
        return ((y % 2), (y // 2), (z % 2), (z // 2) % 2, (z // 4))[4 - level]

    def solve(level, own, sibling):
        side = child_side(level)
        first = jnp.where(side == 0, own, sibling)
        second = jnp.where(side == 0, sibling, own)
        high, low = two_parts(jnp.concatenate([first, second], 1))
        half = pl.ds(pl.multiple_of(side * RANK, RANK), RANK)
        got = dot_nt(jnp.concatenate([high, low], 0), caps[level, 0, half, :])
        rounded = (got[:QUARTER] + got[QUARTER:]).astype(BF16)
        zown[level] = rounded.astype(F32)
        zbuf[level, own_q, :] = rounded.astype(F32)
        return rounded

    p4_out = [message(p4.at[quarter(flips(x, j))], p4_rs.at[j], device(dx=j)) for j in (1, 2, 3)] + [
        message(p4.at[quarter(flips(x, j))], p4_rs.at[4 + j], device(dx=j, dy=1)) for j in range(4)
    ]
    p3_out = [message(p3.at[quarter(flips(x, j))], p3_rs.at[j - 1], device(dx=j)) for j in (1, 2, 3)]
    pr_out = [message(pr.at[quarter(flips(x, j))], pr_rs.at[j - 1], device(dx=j)) for j in (1, 2, 3)]
    e3_out = [message(e3, l3.at[j - 1], device(dy=j)) for j in (1, 2, 3)]
    e2_out = [
        message(e2, l2.at[4 * k + j], device(dy=j, dz=k))
        for k in (0, 1) for j in range(4) if (j, k) != (0, 0)
    ]
    e10_out = [message(e10, l2r.at[j - 1], device(dy=j)) for j in (1, 2, 3)]
    e1_out = [message(e1, l1.at[j - 1], device(dz=j)) for j in (1, 2, 3)]
    f0_out = message(f0, l1r, device(dz=1))
    e0_out = [message(e0, l0.at[i], device(dz=j)) for i, j in enumerate((2, 7, 5))]

    def block(ref, place):
        return ref[:, place * RANK : (place + 1) * RANK]

    @pl.when(core == 1)
    def _():
        proj_pair[0].wait_recv()
        p4[...] += p4_in[...]
        start(p4_out)
        proj_pair[1].wait_recv()
        p3[...] += p3_in[...]
        start(p3_out)
        proj_pair[2].wait_recv()
        pr[...] += pr_in[...]
        start(pr_out)

        wait_recv(p4_out)
        own = p4[own_q, :] + p4_rs[1] + p4_rs[2] + p4_rs[3]
        z4 = solve(4, own, p4_rs[4] + p4_rs[5] + p4_rs[6] + p4_rs[7])
        wait_recv(p3_out)
        wait_recv(gram_out[0])
        own = p3[own_q, :] + p3_rs[0] + p3_rs[1] + p3_rs[2] - times_gram(z4, ga[...])
        e3[...] = own
        start(e3_out)
        start(z_out[4])

        wait_recv(pr_out)
        rest = pr[own_q, :] + pr_rs[0] + pr_rs[1] + pr_rs[2]
        wait_recv(gram_out[1])
        own2 = rest[:, 2 * RANK :] - times_gram(z4, block(gb, 0))
        wait_recv(e3_out)
        z3 = solve(3, own + l3[0], l3[1] + l3[2])
        own2 = own2 - times_gram(z3, block(gb, 1))
        e2[...] = own2
        start(e2_out)
        wait_recv(gram_out[2])
        own10 = rest[:, : 2 * RANK] - times_gram(z4, gc[:, : 2 * RANK])
        own10 = own10 - times_gram(z3, gc[:, 2 * RANK :])
        e10[...] = own10
        start(e10_out)
        start(z_out[3])

        wait_recv(e2_out)
        z2 = solve(2, own2 + l2[1] + l2[2] + l2[3], l2[4] + l2[5] + l2[6] + l2[7])
        wait_recv(e10_out)
        wait_recv(gram_out[3])
        plane = own10 + l2r[0] + l2r[1] + l2r[2] - times_gram(z2, gd[...])
        own1 = plane[:, RANK:]
        e1[...] = own1
        f0[...] = plane[:, :RANK]
        start(e1_out)
        f0_out.start()
        start(z_out[2])

        wait_recv(e1_out)
        z1 = solve(1, own1 + l1[0], l1[1] + l1[2])
        f0_out.wait_recv()
        wait_recv(gram_out[4])
        own0 = plane[:, :RANK] + l1r[...] - times_gram(z1, ge[...])
        e0[...] = own0
        start(e0_out)
        start(z_out[1])
        for level in (4, 3, 2):
            z_wait(level, 1)
        subtract((2, 3, 4))
        wait_recv(e0_out)
        solve(0, own0 + l0[0], l0[1] + l0[2])
        start(z_out[0])
        z_wait(1, 1)
        subtract((1,))
        finish(1)
        for copies in [
            gram_pair, p4_out, p3_out, pr_out, e3_out, e2_out, e10_out, e1_out, [f0_out], e0_out,
        ] + z_out:
            wait_send(copies)

    assert counter[0] <= MESSAGES


MESSAGES = 160


def vmem(*shape, dtype=F32):
    return pltpu.VMEM(shape, dtype)


def tree_solve(loads, inverse, bases, caps):
    rows = loads.shape[0]
    widths = [len(group) * RANK for group in GROUPS]
    q = QUARTER
    scratch = [
        vmem(rows, CASES, dtype=BF16), vmem(rows, rows, dtype=BF16),
        vmem(rows, LEVELS * RANK, dtype=BF16), vmem(*caps.shape, dtype=BF16),
        vmem(rows, CASES), vmem(2 * CASES, LEVELS * RANK),
    ]
    scratch += [vmem(RANK, width) for width in widths] * 2
    scratch += [vmem(3, q, width) for width in widths]
    scratch += [vmem(q, width) for width in widths]
    scratch += [vmem(3, q, widths[3]), vmem(q, 2 * RANK), vmem(q, RANK), vmem(q, RANK), vmem(q, RANK)]
    scratch += [vmem(RANK, width) for width in (RANK, 2 * RANK, 4 * RANK, 2 * RANK, RANK)]
    scratch += [vmem(CASES, width) for width in (RANK, RANK, 3 * RANK)] * 2
    scratch += [vmem(8, q, RANK), vmem(3, q, RANK), vmem(3, q, 3 * RANK)]
    scratch += [vmem(q, RANK), vmem(3, q, RANK), vmem(q, RANK), vmem(8, q, RANK)]
    scratch += [vmem(q, 2 * RANK), vmem(3, q, 2 * RANK), vmem(q, RANK), vmem(3, q, RANK)]
    scratch += [vmem(q, RANK), vmem(q, RANK), vmem(q, RANK), vmem(3, q, RANK)]
    scratch += [vmem(LEVELS, q, RANK), vmem(LEVELS, CASES, RANK)]
    scratch += [
        pltpu.SemaphoreType.DMA((LEVELS + 2,)),
        pltpu.SemaphoreType.DMA((rows // ROWS,)),
        pltpu.SemaphoreType.DMA,
        pltpu.SemaphoreType.DMA((MESSAGES,)),
        pltpu.SemaphoreType.DMA((MESSAGES,)),
    ]
    anywhere = pl.BlockSpec(memory_space=pl.ANY)
    return pl.pallas_call(
        tree_kernel,
        out_shape=(
            jax.ShapeDtypeStruct((rows, CASES), F32),
            jax.ShapeDtypeStruct((CASES, RANK), BF16),
        ),
        in_specs=[anywhere] * 4,
        out_specs=(anywhere, pl.BlockSpec(memory_space=pltpu.VMEM)),
        scratch_shapes=scratch,
        compiler_params=pltpu.CompilerParams(
            collective_id=0, has_side_effects=True, vmem_limit_bytes=50 * 2**20
        ),
        name="tree_solve",
    )(loads, inverse, bases, caps)


def last_kernel(part, basis, z0, out):
    out[...] = part[...] - dot_nt(basis[0], z0[...])


def last_level(part, bases, z0):
    rows = part.shape[0]
    step = rows // 4
    return pl.pallas_call(
        last_kernel,
        grid=(4,),
        out_shape=jax.ShapeDtypeStruct(part.shape, F32),
        in_specs=[
            pl.BlockSpec((step, CASES), lambda i: (i, 0)),
            pl.BlockSpec((1, step, RANK), lambda i: (0, i, 0)),
            pl.BlockSpec((CASES, RANK), lambda i: (0, 0)),
        ],
        out_specs=pl.BlockSpec((step, CASES), lambda i: (i, 0)),
        name="last_level",
    )(part, bases, z0)


def local(loads, leaf_inverse, bases, couplings):
    part, z0 = tree_solve(loads, leaf_inverse, bases, couplings)
    return last_level(part, bases, z0)


def solution(mesh):
    in_specs = (
        P("leaf", None),
        P("leaf", None),
        P(None, "leaf", None),
        P(None, "leaf", None, None),
    )
    return jax.shard_map(
        local, mesh=mesh, in_specs=in_specs, out_specs=P("leaf", None), check_vma=False
    )
```

time: 168 us -> 50.9 us (0.30)
  the two profiles are of different devices: /device:TPU:18 before, /device:TPU:1 now
where the time goes in v1:
time: 50.9 us; the launch traced here: 50.7 us
  Pallas kernels  47 us (92%)
  local copies, waits for them, and re-layouts  3.69 us (7%)
    pallas_call x1, Pallas kernels, tree_solve(): pl.pallas_call(tree_kernel, out_shape=(jax.ShapeDtypeStruct((rows, CASES)...  43.2 us
    pallas_call x1, Pallas kernels, last_level(): pl.pallas_call(last_kernel, grid=(4,), out_shape=jax.ShapeDtypeStruct(par...  3.79 us
    unnamed x8, local copies, waits for them, and re-layouts  3.69 us

profile of v1, /device:TPU:1, one launch (start us, length us, event | category | flops | bytes accessed | tf_op | source)
XLA Modules:
  0.0 50.7 jit_solution(7618940444207687439)
XLA Ops:
  0.0 0.0 copy-start.1
  0.0 1.1 %copy-done.1 = bf16[5,1,256,256]{3,2,1,0:T(8,128)(2,1)S(1)} copy-done((bf16[5,1,256,256]{3,2,1,0:T(8,128)(2,1)S(1)}, bf16[5,1,256,256]{3,2,1,0:T(8,128)(2,1)}, u32[]{:S(2)}) %copy-start.1) | copy-done | bytes 655384
  1.1 0.0 copy-start.2
  1.1 1.0 %copy-done.2 = bf16[2048,128]{1,0:T(8,128)(2,1)S(1)} copy-done((bf16[2048,128]{1,0:T(8,128)(2,1)S(1)}, bf16[2048,128]{1,0:T(8,128)(2,1)}, u32[]{:S(2)}) %copy-start.2) | copy-done | bytes 524312
  2.1 43.2 %tree_solve.1 = (f32[2048,128]{1,0:T(8,128)S(1)}, bf16[128,128]{1,0:T(8,128)(2,1)S(1)}) custom-call(bf16[2048,128]{1,0:T(8,128)(2,1)S(1)} %copy-done.2, bf16[2048,2048]{1,0:T(8,128)(2,1)} %inverse_hbm.1, bf16[5,2048,128]{2,1,0:T(8,128)(2,1)} %basis.1, bf16[5,1,256,256]{3,2,1,0:T(8,128)(2,1)S(1)} %copy-done.1), custom_call_target="tpu_custom_call" | custom-call | tf_op jit(solution)/shard_map/tree_solve/pallas_call | solution.py:445
  45.3 0.0 copy-start
  45.4 1.0 %copy-done = f32[2048,128]{1,0:T(8,128)} copy-done((f32[2048,128]{1,0:T(8,128)}, f32[2048,128]{1,0:T(8,128)S(1)}, u32[]{:S(2)}) %copy-start) | copy-done | bytes 1048600
  46.3 0.0 copy-start.3
  46.3 0.6 %copy-done.3 = bf16[128,128]{1,0:T(8,128)(2,1)} copy-done((bf16[128,128]{1,0:T(8,128)(2,1)}, bf16[128,128]{1,0:T(8,128)(2,1)S(1)}, u32[]{:S(2)}) %copy-start.3) | copy-done | bytes 32792
  46.9 3.8 %last_level.1 = f32[2048,128]{1,0:T(8,128)} custom-call(f32[2048,128]{1,0:T(8,128)} %copy-done, bf16[5,2048,128]{2,1,0:T(8,128)(2,1)} %basis.1, bf16[128,128]{1,0:T(8,128)(2,1)} %copy-done.3), custom_call_target="tpu_custom_call" | custom-call | tf_op jit(solution)/shard_map/last_level/pallas_call | solution.py:468
Async XLA Ops:
  0.0 1.1 %copy-start.1 = (bf16[5,1,256,256]{3,2,1,0:T(8,128)(2,1)S(1)}, bf16[5,1,256,256]{3,2,1,0:T(8,128)(2,1)}, u32[]{:S(2)}) copy-start(bf16[5,1,256,256]{3,2,1,0:T(8,128)(2,1)} %caps_hbm.1) | copy-start | bytes 1966084
  1.1 1.0 %copy-start.2 = (bf16[2048,128]{1,0:T(8,128)(2,1)S(1)}, bf16[2048,128]{1,0:T(8,128)(2,1)}, u32[]{:S(2)}) copy-start(bf16[2048,128]{1,0:T(8,128)(2,1)} %loads_hbm.1) | copy-start | bytes 1572868
  45.3 1.0 %copy-start = (f32[2048,128]{1,0:T(8,128)}, f32[2048,128]{1,0:T(8,128)S(1)}, u32[]{:S(2)}) copy-start(f32[2048,128]{1,0:T(8,128)S(1)} %get-tuple-element.7.part) | copy-start | bytes 3145732
  46.3 0.6 %copy-start.3 = (bf16[128,128]{1,0:T(8,128)(2,1)}, bf16[128,128]{1,0:T(8,128)(2,1)S(1)}, u32[]{:S(2)}) copy-start(bf16[128,128]{1,0:T(8,128)(2,1)S(1)} %get-tuple-element.8.z0) | copy-start | bytes 98308

commit v2 on v0

v2 whole, which is shorter than its diff:
```python
import jax
import jax.numpy as jnp
from jax import lax
from jax.experimental import pallas as pl
from jax.experimental.pallas import tpu as pltpu
from jax.sharding import PartitionSpec as P

MESH = pl.DeviceIdType.MESH
F32 = jnp.float32
BF16 = jnp.bfloat16
RANK = 128
CASES = 128
LEVELS = 5
QUARTER = CASES // 4
ROWS = 512
TILE = 256


def flip(value, bit):
    return value + bit - 2 * bit * ((value // bit) % 2)


def flips(value, mask):
    for bit in (1, 2, 4):
        if mask & bit:
            value = flip(value, bit)
    return value


def dot_tn(a, b):
    return lax.dot_general(a, b, (((0,), (0,)), ((), ())), preferred_element_type=F32)


def dot_nt(a, b):
    return lax.dot_general(a, b, (((1,), (1,)), ((), ())), preferred_element_type=F32)


def two_parts(value):
    high = value.astype(BF16)
    return high, (value - high.astype(F32)).astype(BF16)


def times_gram(*pairs):
    rows, columns = [], []
    for z, gram in pairs:
        rows += [z, z]
        columns += two_parts(gram)
    return jnp.dot(
        jnp.concatenate(rows, 1), jnp.concatenate(columns, 0), preferred_element_type=F32
    )


GROUPS = (
    ((4, 3),),
    ((4, 2), (3, 2)),
    ((4, 1), (3, 1), (2, 1)),
    ((4, 0), (3, 0), (2, 0), (1, 0)),
)
STARTS = (0, RANK, 3 * RANK, 6 * RANK)
WIDTHS = tuple(len(group) * RANK for group in GROUPS)
PIECES = ((0, 3 * RANK), (3 * RANK, 6 * RANK), (6 * RANK, 10 * RANK))


def tree_kernel(
    loads_hbm, inverse_hbm, bases_hbm, caps_hbm,
    out,
    loads, inverse, bcat, caps, field,
    gram, gram_in, sa_rs, sb_rs, sc_rs, sd_rs,
    s43_own, s42_own, s32_own, s41_own, s321_own, s40_own, s310_own, s32_y, s321_y, s310_y,
    t32_own, t321_own, t320_own, t10_own, t10_z, u10_own,
    g43, g42, g32, g41, g321, g40, g320, g10,
    p4, p3, p2, p10, p4_in, p3_in, p2_in, p10_in, p4_rs, p3_rs, p2_rs, p10_rs,
    e3, l3, e2, l2, h1, k1, h0, k0, d2, m2, e1, l1, f0, l1r, e0, l0,
    zown, zbuf,
    local_sem, chunk_sem, send_sem, recv_sem,
):
    rows = field.shape[0]
    steps = rows // ROWS
    me = lax.axis_index("leaf")
    core = me % 2
    x = (me // 2) % 4
    y = (me // 8) % 4
    z = me // 32

    def device(dx=0, dy=0, dz=0, on=1):
        return ((flips(z, dz) * 4 + flips(y, dy)) * 4 + flips(x, dx)) * 2 + on

    loads_in = []
    for level in range(LEVELS):
        copy = pltpu.make_async_copy(
            bases_hbm.at[level], bcat.at[:, pl.ds(level * RANK, RANK)], local_sem.at[level]
        )
        copy.start()
        loads_in.append(copy)
    loads_copy = pltpu.make_async_copy(loads_hbm, loads, local_sem.at[LEVELS])
    loads_copy.start()
    caps_copy = pltpu.make_async_copy(caps_hbm, caps, local_sem.at[LEVELS + 1])

    def inverse_copy(step):
        part = pl.ds(pl.multiple_of(step * ROWS, ROWS), ROWS)
        return pltpu.make_async_copy(inverse_hbm.at[part], inverse.at[part], chunk_sem.at[step])

    for step in range(steps):
        inverse_copy(step).start()
    caps_copy.start()

    barrier = pltpu.get_barrier_semaphore()

    def greet(partners):
        for partner in partners:
            pl.semaphore_signal(barrier, inc=1, device_id=(partner,), device_id_type=MESH)

    gram_partners = (
        [device(dx=j, on=0) for j in (1, 2, 3)]
        + [device(dy=j, on=0) for j in (1, 2, 3)]
        + [device(dz=1, on=0)]
        + [device(dx=j, on=1) for j in range(4)]
    )
    chain_partners = (
        [device(dx=j, on=0) for j in range(4)]
        + [device(dx=j) for j in (1, 2, 3)]
        + [device(dx=j, dy=1) for j in range(4)]
        + [device(dy=j) for j in (2, 3)]
        + [device(dy=j, dz=1) for j in range(4)]
        + [device(dz=j) for j in (2, 3, 7, 5)]
    )

    @pl.when(core == 0)
    def _():
        greet(gram_partners)

    @pl.when(core == 1)
    def _():
        greet(chain_partners)

    with jax.named_scope("bases_in"):
        for copy in loads_in:
            copy.wait()
    with jax.named_scope("gram_blocks"):
        for level in (4, 3, 2, 1):
            got = dot_tn(bcat[:, level * RANK : (level + 1) * RANK], bcat[:, : level * RANK])
            for begin, group in zip(STARTS, GROUPS):
                for place, (source, target) in enumerate(group):
                    if source == level:
                        at = begin + place * RANK
                        gram[:, at : at + RANK] = got[:, target * RANK : (target + 1) * RANK]

    @pl.when(core == 0)
    def _():
        with jax.named_scope("meet"):
            pl.semaphore_wait(barrier, len(gram_partners))

    @pl.when(core == 1)
    def _():
        with jax.named_scope("meet"):
            pl.semaphore_wait(barrier, len(chain_partners))

    counter = [0]

    class Stage:
        def __init__(self, name, copies, arrive, leave=None):
            self.name = name
            self.number = counter[0]
            counter[0] += 1
            self.copies = copies
            self.arrive = arrive
            self.leave = arrive if leave is None else leave

        def describe(self, src, dst, target):
            return pltpu.make_async_remote_copy(
                src_ref=src, dst_ref=dst,
                send_sem=send_sem.at[self.number], recv_sem=recv_sem.at[self.number],
                device_id=(target,), device_id_type=MESH,
            )

        def start(self):
            for copy in self.copies:
                self.describe(*copy).start()

        def wait_recv(self, arrive=None):
            ref = self.arrive if arrive is None else arrive
            with jax.named_scope("wait_" + self.name):
                self.describe(ref, ref, self.copies[0][2]).wait_recv()

        def wait_send(self):
            self.describe(self.leave, self.leave, self.copies[0][2]).wait_send()

    def quarter(index):
        return pl.ds(pl.multiple_of(index * QUARTER, QUARTER), QUARTER)

    other = device(on=1 - core)
    gram_pair = [
        Stage("gram_in", [(gram.at[:, low:high], gram_in.at[:, low:high], other)], gram_in.at[:, low:high])
        for low, high in PIECES
    ]

    @pl.when(core == 1)
    def _():
        for stage in gram_pair:
            stage.start()

    loads_copy.wait()

    def field_step(step):
        with jax.named_scope("inverse_in"):
            inverse_copy(step).wait()
        with jax.named_scope("field"):
            for begin in range(step * ROWS, (step + 1) * ROWS, TILE):
                part = pl.ds(begin, TILE)
                field[part, :] = jnp.dot(inverse[part, :], loads[...], preferred_element_type=F32)

    field_step(0)

    rs_slots = (sa_rs, sb_rs, sc_rs, sd_rs)
    gram_rs = [
        Stage(
            "gram_row",
            [
                (gram.at[quarter(flips(x, j)), pl.ds(begin, width)], slots.at[j - 1], device(dx=j, on=0))
                for j in (1, 2, 3)
            ],
            slots,
        )
        for begin, width, slots in zip(STARTS, WIDTHS, rs_slots)
    ]

    def pair_sum(piece):
        with jax.named_scope("pair_sums"):
            low, high = PIECES[piece]
            gram_pair[piece].wait_recv()
            gram[:, low:high] += gram_in[:, low:high]

    @pl.when(core == 0)
    def _():
        pair_sum(0)
        gram_rs[0].start()
        gram_rs[1].start()

    field_step(1)

    @pl.when(core == 0)
    def _():
        pair_sum(1)
        gram_rs[2].start()

    field_step(2)

    @pl.when(core == 0)
    def _():
        pair_sum(2)
        gram_rs[3].start()

    for step in range(3, steps):
        field_step(step)

    ordered = (p4, p3, p2, p10)
    with jax.named_scope("projections"):
        field_b = field[...].astype(BF16)
        got = dot_tn(field_b, bcat[:, 3 * RANK :])
        p4[...] = got[:, RANK:]
        p3[...] = got[:, :RANK]
    ordered_in = (p4_in, p3_in, p2_in, p10_in)
    proj_pair = [Stage("proj_in", [(src, dst, other)], dst) for src, dst in zip(ordered, ordered_in)]
    own_q = quarter(x)

    @pl.when(core == 0)
    def _():
        proj_pair[0].start()
        proj_pair[1].start()

    with jax.named_scope("projections_rest"):
        got = dot_tn(field_b, bcat[:, : 3 * RANK])
        p2[...] = got[:, 2 * RANK :]
        p10[...] = got[:, : 2 * RANK]

    z_targets = [(j, on) for on in (0, 1) for j in range(4) if (j, on) != (0, 1)]
    z_out = [
        Stage(
            "z%d" % level,
            [(zown.at[level], zbuf.at[level, own_q], device(dx=j, on=on)) for j, on in z_targets],
            zbuf.at[level], p4_rs,
        )
        for level in range(LEVELS)
    ]

    def z_wait(level, on):
        z_out[level].wait_recv(zbuf.at[level, pl.ds(0, (4 - on) * QUARTER)])

    def subtract(levels, into):
        factors = jnp.concatenate([zbuf[level].astype(BF16) for level in levels], 1)
        low, high = levels[0] * RANK, (levels[-1] + 1) * RANK
        for step in range(steps):
            part = pl.ds(step * ROWS, ROWS)
            into[part, :] = field[part, :] - dot_nt(bcat[part, low:high], factors)

    caps_copy.wait()

    gram_out = {
        name: Stage("gram_" + name, [(src, dst.at[own_q], device(dx=j)) for j in range(4)], dst)
        for name, src, dst in (
            ("43", s43_own, g43), ("42", s42_own, g42), ("32", t32_own, g32), ("41", s41_own, g41),
            ("321", t321_own, g321), ("40", s40_own, g40), ("320", t320_own, g320), ("10", u10_own, g10),
        )
    }
    plane_out = {
        name: Stage("plane" + name, [(src, dst.at[j - 1], device(dy=j, on=0)) for j in (1, 2, 3)], dst)
        for name, src, dst in (("32", s32_own, s32_y), ("321", s321_own, s321_y), ("310", s310_own, s310_y))
    }
    pair_out = Stage("pair", [(t10_own, t10_z, device(dz=1, on=0))], t10_z)

    def row_sum(group):
        gram_rs[group].wait_recv()
        slots = rs_slots[group]
        begin, width = STARTS[group], WIDTHS[group]
        return gram[own_q, begin : begin + width] + slots[0] + slots[1] + slots[2]

    @pl.when(core == 0)
    def _():
        proj_pair[2].start()
        proj_pair[3].start()
        with jax.named_scope("gram_a"):
            s43_own[...] = row_sum(0)
            gram_out["43"].start()
        with jax.named_scope("gram_b"):
            got = row_sum(1)
            s42_own[...] = got[:, :RANK]
            s32_own[...] = got[:, RANK:]
            plane_out["32"].start()
            gram_out["42"].start()
        with jax.named_scope("gram_c"):
            got = row_sum(2)
            s41_own[...] = got[:, :RANK]
            s321_own[...] = got[:, RANK:]
            plane_out["321"].start()
            gram_out["41"].start()
        with jax.named_scope("gram_d"):
            got = row_sum(3)
            s40_own[...] = got[:, :RANK]
            s310_own[...] = got[:, RANK:]
            plane_out["310"].start()
            gram_out["40"].start()
        with jax.named_scope("gram_plane32"):
            plane_out["32"].wait_recv()
            t32_own[:, :RANK] = s32_own[...] + s32_y[0]
            t32_own[:, RANK:] = s32_y[1] + s32_y[2]
            gram_out["32"].start()
        with jax.named_scope("gram_plane321"):
            plane_out["321"].wait_recv()
            near = s321_own[...] + s321_y[0]
            far = s321_y[1] + s321_y[2]
            t321_own[:, :RANK] = near[:, :RANK]
            t321_own[:, RANK : 2 * RANK] = far[:, :RANK]
            t321_own[:, 2 * RANK :] = near[:, RANK:] + far[:, RANK:]
            gram_out["321"].start()
        with jax.named_scope("gram_plane310"):
            plane_out["310"].wait_recv()
            near = s310_own[...] + s310_y[0]
            far = s310_y[1] + s310_y[2]
            total = near[:, RANK:] + far[:, RANK:]
            t10_own[...] = total[:, RANK:]
            pair_out.start()
            t320_own[:, :RANK] = near[:, :RANK]
            t320_own[:, RANK : 2 * RANK] = far[:, :RANK]
            t320_own[:, 2 * RANK :] = total[:, :RANK]
            gram_out["320"].start()
        with jax.named_scope("gram_pair"):
            pair_out.wait_recv()
            u10_own[...] = t10_own[...] + t10_z[...]
            gram_out["10"].start()
        with jax.named_scope("field_update"):
            for level in (4, 3, 2):
                z_wait(level, 0)
            subtract((2, 3, 4), field)
            z_wait(1, 0)
            subtract((1,), field)
            z_wait(0, 0)
            subtract((0,), out)
        with jax.named_scope("sent"):
            for stage in (
                gram_rs + list(gram_out.values()) + list(plane_out.values()) + [pair_out] + proj_pair
            ):
                stage.wait_send()

    def child_side(level):
        return ((y % 2), (y // 2), (z % 2), (z // 2) % 2, (z // 4))[4 - level]

    def solve(level, own, sibling):
        side = child_side(level)
        first = jnp.where(side == 0, own, sibling)
        second = jnp.where(side == 0, sibling, own)
        high, low = two_parts(jnp.concatenate([first, second], 1))
        got = dot_nt(jnp.concatenate([high, low], 0), caps[level, 0])
        rounded = (got[:QUARTER] + got[QUARTER:]).astype(BF16)
        left, right = rounded[:, :RANK], rounded[:, RANK:]
        near = jnp.where(side == 0, left, right)
        far = jnp.where(side == 0, right, left)
        zown[level] = near.astype(F32)
        zbuf[level, own_q, :] = near.astype(F32)
        return near, far

    p4_out = Stage(
        "p4",
        [(p4.at[quarter(flips(x, j))], p4_rs.at[j - 1], device(dx=j)) for j in (1, 2, 3)]
        + [(p4.at[quarter(flips(x, j))], p4_rs.at[3 + j], device(dx=j, dy=1)) for j in range(4)],
        p4_rs,
    )
    p3_out, p2_out, p10_out = [
        Stage(name, [(src.at[quarter(flips(x, j))], slots.at[j - 1], device(dx=j)) for j in (1, 2, 3)], slots)
        for name, src, slots in (("p3", p3, p3_rs), ("p2", p2, p2_rs), ("p10", p10, p10_rs))
    ]
    e3_out = Stage("e3", [(e3, l3.at[j - 1], device(dy=j)) for j in (1, 2, 3)], l3)
    e2_out = Stage("e2", [(e2, l2.at[j - 1], device(dy=j)) for j in (1, 2, 3)], l2)
    h1_out = Stage("h1", [(h1, k1.at[j - 1], device(dy=j)) for j in (1, 2, 3)], k1)
    h0_out = Stage("h0", [(h0, k0.at[j - 1], device(dy=j)) for j in (1, 2, 3)], k0)
    d2_out = Stage("d2", [(d2, m2, device(dz=1))], m2)
    e1_out = Stage("e1", [(e1, l1.at[j - 1], device(dz=j)) for j in (1, 2, 3)], l1)
    f0_out = Stage("f0", [(f0, l1r, device(dz=1))], l1r)
    e0_out = Stage("e0", [(e0, l0.at[i], device(dz=j)) for i, j in enumerate((2, 7, 5))], l0)

    @pl.when(core == 1)
    def _():
        with jax.named_scope("proj_pair"):
            for stage, ref, arrived, onward in zip(
                proj_pair, ordered, ordered_in, (p4_out, p3_out, p2_out, p10_out)
            ):
                stage.wait_recv()
                ref[...] += arrived[...]
                onward.start()

        with jax.named_scope("level4"):
            p4_out.wait_recv()
            own = p4[own_q, :] + p4_rs[0] + p4_rs[1] + p4_rs[2]
            z4, _ = solve(4, own, p4_rs[3] + p4_rs[4] + p4_rs[5] + p4_rs[6])
        with jax.named_scope("correct_by_4"):
            p3_out.wait_recv()
            gram_out["43"].wait_recv()
            own3 = p3[own_q, :] + p3_rs[0] + p3_rs[1] + p3_rs[2] - times_gram((z4, g43[...]))
            e3[...] = own3
            e3_out.start()
            p2_out.wait_recv()
            gram_out["42"].wait_recv()
            own2 = p2[own_q, :] + p2_rs[0] + p2_rs[1] + p2_rs[2] - times_gram((z4, g42[...]))
            e2[...] = own2
            e2_out.start()
            p10_out.wait_recv()
            own10 = p10[own_q, :] + p10_rs[0] + p10_rs[1] + p10_rs[2]
            gram_out["41"].wait_recv()
            own1 = own10[:, RANK:] - times_gram((z4, g41[...]))
            h1[...] = own1
            h1_out.start()
            gram_out["40"].wait_recv()
            own0 = own10[:, :RANK] - times_gram((z4, g40[...]))
            h0[...] = own0
            h0_out.start()
            z_out[4].start()
        with jax.named_scope("level3"):
            e3_out.wait_recv()
            z3, y3 = solve(3, own3 + l3[0], l3[1] + l3[2])
        with jax.named_scope("correct_by_3"):
            e2_out.wait_recv()
            plane2 = own2 + l2[0] + l2[1] + l2[2]
            gram_out["32"].wait_recv()
            plane2 = plane2 - times_gram((z3, g32[:, :RANK]), (y3, g32[:, RANK:]))
            d2[...] = plane2
            d2_out.start()
            z_out[3].start()
            h1_out.wait_recv()
            plane1 = own1 + k1[0] + k1[1] + k1[2]
        with jax.named_scope("level2"):
            d2_out.wait_recv()
            z2, _ = solve(2, plane2, m2[...])
            gram_out["321"].wait_recv()
            plane1 = plane1 - times_gram(
                (z3, g321[:, :RANK]), (y3, g321[:, RANK : 2 * RANK]), (z2, g321[:, 2 * RANK :])
            )
            e1[...] = plane1
            e1_out.start()
        with jax.named_scope("correct_0"):
            h0_out.wait_recv()
            gram_out["320"].wait_recv()
            plane0 = own0 + k0[0] + k0[1] + k0[2] - times_gram(
                (z3, g320[:, :RANK]), (y3, g320[:, RANK : 2 * RANK]), (z2, g320[:, 2 * RANK :])
            )
            f0[...] = plane0
            f0_out.start()
            z_out[2].start()
        with jax.named_scope("level1"):
            e1_out.wait_recv()
            z1, _ = solve(1, plane1 + l1[0], l1[1] + l1[2])
        with jax.named_scope("correct_by_1"):
            f0_out.wait_recv()
            gram_out["10"].wait_recv()
            pair0 = plane0 + l1r[...] - times_gram((z1, g10[...]))
            e0[...] = pair0
            e0_out.start()
            z_out[1].start()
            for level in (4, 3, 2):
                z_wait(level, 1)
            subtract((2, 3, 4), field)
        with jax.named_scope("level0"):
            e0_out.wait_recv()
            solve(0, pair0 + l0[0], l0[1] + l0[2])
            z_out[0].start()
        with jax.named_scope("field_update"):
            z_wait(1, 1)
            subtract((1,), field)
            z_wait(0, 1)
            subtract((0,), out)
        with jax.named_scope("sent"):
            for stage in gram_pair + [
                p4_out, p3_out, p2_out, p10_out, e3_out, e2_out, h1_out, h0_out, d2_out, e1_out, f0_out, e0_out,
            ] + z_out:
                stage.wait_send()

    assert counter[0] == STAGES


STAGES = 40


def vmem(*shape, dtype=F32):
    return pltpu.VMEM(shape, dtype)


def tree_solve(loads, inverse, bases, caps):
    rows = loads.shape[0]
    q = QUARTER
    scratch = [
        vmem(rows, CASES, dtype=BF16), vmem(rows, rows, dtype=BF16),
        vmem(rows, LEVELS * RANK, dtype=BF16), vmem(*caps.shape, dtype=BF16),
        vmem(rows, CASES),
    ]
    scratch += [vmem(RANK, sum(WIDTHS))] * 2
    scratch += [vmem(3, q, width) for width in WIDTHS]
    scratch += [vmem(q, width * RANK) for width in (1, 1, 1, 1, 2, 1, 3)]
    scratch += [vmem(3, q, width * RANK) for width in (1, 2, 3)]
    scratch += [vmem(q, width * RANK) for width in (2, 3, 3, 1, 1, 1)]
    scratch += [vmem(RANK, width * RANK) for width in (1, 1, 2, 1, 3, 1, 3, 1)]
    scratch += [vmem(CASES, width * RANK) for width in (1, 1, 1, 2)] * 2
    scratch += [vmem(7, q, RANK), vmem(3, q, RANK), vmem(3, q, RANK), vmem(3, q, 2 * RANK)]
    scratch += [vmem(q, RANK), vmem(3, q, RANK)] * 4
    scratch += [vmem(q, RANK), vmem(q, RANK)]
    scratch += [vmem(q, RANK), vmem(3, q, RANK), vmem(q, RANK), vmem(q, RANK), vmem(q, RANK), vmem(3, q, RANK)]
    scratch += [vmem(LEVELS, q, RANK), vmem(LEVELS, CASES, RANK)]
    scratch += [
        pltpu.SemaphoreType.DMA((LEVELS + 2,)),
        pltpu.SemaphoreType.DMA((rows // ROWS,)),
        pltpu.SemaphoreType.DMA((STAGES,)),
        pltpu.SemaphoreType.DMA((STAGES,)),
    ]
    anywhere = pl.BlockSpec(memory_space=pl.ANY)
    return pl.pallas_call(
        tree_kernel,
        out_shape=pltpu.VMEM((rows, CASES), F32),
        in_specs=[anywhere] * 4,
        out_specs=pl.BlockSpec(memory_space=pltpu.VMEM),
        scratch_shapes=scratch,
        compiler_params=pltpu.CompilerParams(
            collective_id=0, has_side_effects=True, vmem_limit_bytes=60 * 2**20
        ),
        name="tree_solve",
    )(loads, inverse, bases, caps)


def local(loads, leaf_inverse, bases, couplings):
    return tree_solve(loads, leaf_inverse, bases, couplings)


def solution(mesh):
    in_specs = (
        P("leaf", None),
        P("leaf", None),
        P(None, "leaf", None),
        P(None, "leaf", None, None),
    )
    return jax.shard_map(
        local, mesh=mesh, in_specs=in_specs, out_specs=P("leaf", None), check_vma=False
    )
```

time: 168 us -> 40.2 us (0.24)
  the two profiles are of different devices: /device:TPU:18 before, /device:TPU:1 now
where the time goes in v2:
time: 40.2 us; the launch traced here: 40.1 us
  Pallas kernels  39.1 us (97%)
  local copies, waits for them, and re-layouts  0.97 us (2%)
    pallas_call x1, Pallas kernels, tree_solve(): pl.pallas_call(tree_kernel, out_shape=pltpu.VMEM((rows, CASES), F32), in_...  39.1 us
    unnamed x1, local copies, waits for them, and re-layouts  0.97 us

profile of v2, /device:TPU:1, one launch (start us, length us, event | category | flops | bytes accessed | tf_op | source)
XLA Modules:
  0.0 40.1 jit_solution(65974270168101930)
XLA Ops:
  0.0 39.1 %tree_solve.1 = f32[2048,128]{1,0:T(8,128)S(1)} custom-call(bf16[2048,128]{1,0:T(8,128)(2,1)} %loads_hbm.1, bf16[2048,2048]{1,0:T(8,128)(2,1)} %inverse_hbm.1, bf16[5,2048,128]{2,1,0:T(8,128)(2,1)} %bases_hbm.1, bf16[5,1,256,256]{3,2,1,0:T(8,128)(2,1)} %caps_hbm.1), custom_call_target="tpu_custom_call" | custom-call | tf_op jit(solution)/shard_map/tree_solve/pallas_call | solution.py:552
  39.1 1.0 %copy.6 = f32[2048,128]{1,0:T(8,128)} copy(f32[2048,128]{1,0:T(8,128)S(1)} %tree_solve.1) | data formatting | bytes 2097152

commit v3 on v2

--- a/solution.py
+++ b/solution.py
@@ -51,14 +51,14 @@
 
 
 GROUPS = (
-    ((4, 3),),
+    ((4, 3), (1, 0)),
     ((4, 2), (3, 2)),
     ((4, 1), (3, 1), (2, 1)),
-    ((4, 0), (3, 0), (2, 0), (1, 0)),
+    ((4, 0), (3, 0), (2, 0)),
 )
-STARTS = (0, RANK, 3 * RANK, 6 * RANK)
+STARTS = (0, 2 * RANK, 4 * RANK, 7 * RANK)
 WIDTHS = tuple(len(group) * RANK for group in GROUPS)
-PIECES = ((0, 3 * RANK), (3 * RANK, 6 * RANK), (6 * RANK, 10 * RANK))
+PIECES = ((0, 4 * RANK), (4 * RANK, 7 * RANK), (7 * RANK, 10 * RANK))
 
 
 def tree_kernel(
@@ -66,12 +66,12 @@
     out,
     loads, inverse, bcat, caps, field,
     gram, gram_in, sa_rs, sb_rs, sc_rs, sd_rs,
-    s43_own, s42_own, s32_own, s41_own, s321_own, s40_own, s310_own, s32_y, s321_y, s310_y,
+    s43_own, s42_own, s32_own, s41_own, s321_own, s40_own, s10_own, s320_own, s32_y, s321_y, s10_y, s320_y,
     t32_own, t321_own, t320_own, t10_own, t10_z, u10_own,
     g43, g42, g32, g41, g321, g40, g320, g10,
     p4, p3, p2, p10, p4_in, p3_in, p2_in, p10_in, p4_rs, p3_rs, p2_rs, p10_rs,
-    e3, l3, e2, l2, h1, k1, h0, k0, d2, m2, e1, l1, f0, l1r, e0, l0,
-    zown, zbuf,
+    e3, l3, e2, l2, h1, k1, h0, k0, d2, m2, e1, l1, f0, l1r, e0, l0, e0_sent,
+    zown, zbuf, z_sent,
     local_sem, chunk_sem, send_sem, recv_sem,
 ):
     rows = field.shape[0]
@@ -100,10 +100,6 @@
         part = pl.ds(pl.multiple_of(step * ROWS, ROWS), ROWS)
         return pltpu.make_async_copy(inverse_hbm.at[part], inverse.at[part], chunk_sem.at[step])
 
-    for step in range(steps):
-        inverse_copy(step).start()
-    caps_copy.start()
-
     barrier = pltpu.get_barrier_semaphore()
 
     def greet(partners):
@@ -113,7 +109,7 @@
     gram_partners = (
         [device(dx=j, on=0) for j in (1, 2, 3)]
         + [device(dy=j, on=0) for j in (1, 2, 3)]
-        + [device(dz=1, on=0)]
+        + [device(dz=j, on=0) for j in (1, 2, 3)]
         + [device(dx=j, on=1) for j in range(4)]
     )
     chain_partners = (
@@ -121,8 +117,7 @@
         + [device(dx=j) for j in (1, 2, 3)]
         + [device(dx=j, dy=1) for j in range(4)]
         + [device(dy=j) for j in (2, 3)]
-        + [device(dy=j, dz=1) for j in range(4)]
-        + [device(dz=j) for j in (2, 3, 7, 5)]
+        + [device(dz=j) for j in (1, 2, 3, 6, 7)]
     )
 
     @pl.when(core == 0)
@@ -132,6 +127,10 @@
     @pl.when(core == 1)
     def _():
         greet(chain_partners)
+
+    for step in range(steps):
+        inverse_copy(step).start()
+    caps_copy.start()
 
     with jax.named_scope("bases_in"):
         for copy in loads_in:
@@ -169,7 +168,7 @@
         def describe(self, src, dst, target):
             return pltpu.make_async_remote_copy(
                 src_ref=src, dst_ref=dst,
-                send_sem=send_sem.at[self.number], recv_sem=recv_sem.at[self.number],
+                send_sem=send_sem, recv_sem=recv_sem.at[self.number],
                 device_id=(target,), device_id_type=MESH,
             )
 
@@ -217,7 +216,7 @@
             "gram_row",
             [
                 (gram.at[quarter(flips(x, j)), pl.ds(begin, width)], slots.at[j - 1], device(dx=j, on=0))
-                for j in (1, 2, 3)
+                for j in (2, 3, 1)
             ],
             slots,
         )
@@ -242,15 +241,10 @@
     def _():
         pair_sum(1)
         gram_rs[2].start()
-
-    field_step(2)
-
-    @pl.when(core == 0)
-    def _():
         pair_sum(2)
         gram_rs[3].start()
 
-    for step in range(3, steps):
+    for step in range(2, steps):
         field_step(step)
 
     ordered = (p4, p3, p2, p10)
@@ -268,23 +262,37 @@
         proj_pair[0].start()
         proj_pair[1].start()
 
-    with jax.named_scope("projections_rest"):
-        got = dot_tn(field_b, bcat[:, : 3 * RANK])
-        p2[...] = got[:, 2 * RANK :]
-        p10[...] = got[:, : 2 * RANK]
-
-    z_targets = [(j, on) for on in (0, 1) for j in range(4) if (j, on) != (0, 1)]
-    z_out = [
-        Stage(
-            "z%d" % level,
-            [(zown.at[level], zbuf.at[level, own_q], device(dx=j, on=on)) for j, on in z_targets],
-            zbuf.at[level], p4_rs,
+    with jax.named_scope("projection_2"):
+        p2[...] = dot_tn(field_b, bcat[:, 2 * RANK : 3 * RANK])
+
+    @pl.when(core == 0)
+    def _():
+        proj_pair[2].start()
+
+    with jax.named_scope("projections_10"):
+        p10[...] = dot_tn(field_b, bcat[:, : 2 * RANK])
+
+    @pl.when(core == 0)
+    def _():
+        proj_pair[3].start()
+
+    z_targets = [(j, on) for on in (0, 1) for j in (2, 3, 1, 0) if (j, on) != (0, 1)]
+
+    def z_stage(low, high):
+        levels = pl.ds(low, high - low)
+        return Stage(
+            "z%d" % low,
+            [
+                (zown.at[levels], zbuf.at[levels, own_q], device(dx=j, on=on))
+                for j, on in z_targets
+            ],
+            zbuf.at[levels], z_sent.at[levels],
         )
-        for level in range(LEVELS)
-    ]
-
-    def z_wait(level, on):
-        z_out[level].wait_recv(zbuf.at[level, pl.ds(0, (4 - on) * QUARTER)])
+
+    z_low, z_one, z_rest = z_stage(0, 1), z_stage(1, 2), z_stage(2, 5)
+
+    def z_wait(stage, low, high, on):
+        stage.wait_recv(zbuf.at[pl.ds(low, high - low), pl.ds(0, (4 - on) * QUARTER)])
 
     def subtract(levels, into):
         factors = jnp.concatenate([zbuf[level].astype(BF16) for level in levels], 1)
@@ -296,7 +304,7 @@
     caps_copy.wait()
 
     gram_out = {
-        name: Stage("gram_" + name, [(src, dst.at[own_q], device(dx=j)) for j in range(4)], dst)
+        name: Stage("gram_" + name, [(src, dst.at[own_q], device(dx=j)) for j in (2, 3, 1, 0)], dst)
         for name, src, dst in (
             ("43", s43_own, g43), ("42", s42_own, g42), ("32", t32_own, g32), ("41", s41_own, g41),
             ("321", t321_own, g321), ("40", s40_own, g40), ("320", t320_own, g320), ("10", u10_own, g10),
@@ -304,9 +312,9 @@
     }
     plane_out = {
         name: Stage("plane" + name, [(src, dst.at[j - 1], device(dy=j, on=0)) for j in (1, 2, 3)], dst)
-        for name, src, dst in (("32", s32_own, s32_y), ("321", s321_own, s321_y), ("310", s310_own, s310_y))
+        for name, src, dst in (("32", s32_own, s32_y), ("321", s321_own, s321_y), ("10", s10_own, s10_y), ("320", s320_own, s320_y))
     }
-    pair_out = Stage("pair", [(t10_own, t10_z, device(dz=1, on=0))], t10_z)
+    pair_out = Stage("pair", [(t10_own, t10_z.at[j - 1], device(dz=j, on=0)) for j in (3, 2, 1)], t10_z)
 
     def row_sum(group):
         gram_rs[group].wait_recv()
@@ -316,11 +324,12 @@
 
     @pl.when(core == 0)
     def _():
-        proj_pair[2].start()
-        proj_pair[3].start()
         with jax.named_scope("gram_a"):
-            s43_own[...] = row_sum(0)
+            got = row_sum(0)
+            s43_own[...] = got[:, :RANK]
+            s10_own[...] = got[:, RANK:]
             gram_out["43"].start()
+            plane_out["10"].start()
         with jax.named_scope("gram_b"):
             got = row_sum(1)
             s42_own[...] = got[:, :RANK]
@@ -336,9 +345,13 @@
         with jax.named_scope("gram_d"):
             got = row_sum(3)
             s40_own[...] = got[:, :RANK]
-            s310_own[...] = got[:, RANK:]
-            plane_out["310"].start()
+            s320_own[...] = got[:, RANK:]
+            plane_out["320"].start()
             gram_out["40"].start()
+        with jax.named_scope("gram_plane10"):
+            plane_out["10"].wait_recv()
+            t10_own[...] = s10_own[...] + s10_y[0] + s10_y[1] + s10_y[2]
+            pair_out.start()
         with jax.named_scope("gram_plane32"):
             plane_out["32"].wait_recv()
             t32_own[:, :RANK] = s32_own[...] + s32_y[0]
@@ -352,28 +365,24 @@
             t321_own[:, RANK : 2 * RANK] = far[:, :RANK]
             t321_own[:, 2 * RANK :] = near[:, RANK:] + far[:, RANK:]
             gram_out["321"].start()
-        with jax.named_scope("gram_plane310"):
-            plane_out["310"].wait_recv()
-            near = s310_own[...] + s310_y[0]
-            far = s310_y[1] + s310_y[2]
-            total = near[:, RANK:] + far[:, RANK:]
-            t10_own[...] = total[:, RANK:]
-            pair_out.start()
+        with jax.named_scope("gram_plane320"):
+            plane_out["320"].wait_recv()
+            near = s320_own[...] + s320_y[0]
+            far = s320_y[1] + s320_y[2]
             t320_own[:, :RANK] = near[:, :RANK]
             t320_own[:, RANK : 2 * RANK] = far[:, :RANK]
-            t320_own[:, 2 * RANK :] = total[:, :RANK]
+            t320_own[:, 2 * RANK :] = near[:, RANK:] + far[:, RANK:]
             gram_out["320"].start()
         with jax.named_scope("gram_pair"):
             pair_out.wait_recv()
-            u10_own[...] = t10_own[...] + t10_z[...]
+            u10_own[:, :RANK] = t10_own[...] + t10_z[0]
+            u10_own[:, RANK:] = t10_z[1] + t10_z[2]
             gram_out["10"].start()
         with jax.named_scope("field_update"):
-            for level in (4, 3, 2):
-                z_wait(level, 0)
-            subtract((2, 3, 4), field)
-            z_wait(1, 0)
-            subtract((1,), field)
-            z_wait(0, 0)
+            z_wait(z_rest, 2, 5, 0)
+            z_wait(z_one, 1, 2, 0)
+            subtract((1, 2, 3, 4), field)
+            z_wait(z_low, 0, 1, 0)
             subtract((0,), out)
         with jax.named_scope("sent"):
             for stage in (
@@ -400,12 +409,12 @@
 
     p4_out = Stage(
         "p4",
-        [(p4.at[quarter(flips(x, j))], p4_rs.at[j - 1], device(dx=j)) for j in (1, 2, 3)]
-        + [(p4.at[quarter(flips(x, j))], p4_rs.at[3 + j], device(dx=j, dy=1)) for j in range(4)],
+        [(p4.at[quarter(flips(x, j))], p4_rs.at[j - 1], device(dx=j)) for j in (2, 3, 1)]
+        + [(p4.at[quarter(flips(x, j))], p4_rs.at[3 + j], device(dx=j, dy=1)) for j in (2, 3, 1, 0)],
         p4_rs,
     )
     p3_out, p2_out, p10_out = [
-        Stage(name, [(src.at[quarter(flips(x, j))], slots.at[j - 1], device(dx=j)) for j in (1, 2, 3)], slots)
+        Stage(name, [(src.at[quarter(flips(x, j))], slots.at[j - 1], device(dx=j)) for j in (2, 3, 1)], slots)
         for name, src, slots in (("p3", p3, p3_rs), ("p2", p2, p2_rs), ("p10", p10, p10_rs))
     ]
     e3_out = Stage("e3", [(e3, l3.at[j - 1], device(dy=j)) for j in (1, 2, 3)], l3)
@@ -413,9 +422,10 @@
     h1_out = Stage("h1", [(h1, k1.at[j - 1], device(dy=j)) for j in (1, 2, 3)], k1)
     h0_out = Stage("h0", [(h0, k0.at[j - 1], device(dy=j)) for j in (1, 2, 3)], k0)
     d2_out = Stage("d2", [(d2, m2, device(dz=1))], m2)
-    e1_out = Stage("e1", [(e1, l1.at[j - 1], device(dz=j)) for j in (1, 2, 3)], l1)
-    f0_out = Stage("f0", [(f0, l1r, device(dz=1))], l1r)
-    e0_out = Stage("e0", [(e0, l0.at[i], device(dz=j)) for i, j in enumerate((2, 7, 5))], l0)
+    e1_out = Stage("e1", [(e1, l1.at[j - 1], device(dz=j)) for j in (3, 2, 1)], l1)
+    f0_out = Stage("f0", [(f0, l1r.at[j - 1], device(dz=j)) for j in (3, 2, 1)], l1r)
+    at_end = (z % 4) * (3 - z % 4) == 0
+    e0_out = Stage("e0", [(e0, l0, device(dz=j)) for j in (6, 7)], l0, e0_sent)
 
     @pl.when(core == 1)
     def _():
@@ -452,7 +462,6 @@
             own0 = own10[:, :RANK] - times_gram((z4, g40[...]))
             h0[...] = own0
             h0_out.start()
-            z_out[4].start()
         with jax.named_scope("level3"):
             e3_out.wait_recv()
             z3, y3 = solve(3, own3 + l3[0], l3[1] + l3[2])
@@ -463,16 +472,15 @@
             plane2 = plane2 - times_gram((z3, g32[:, :RANK]), (y3, g32[:, RANK:]))
             d2[...] = plane2
             d2_out.start()
-            z_out[3].start()
             h1_out.wait_recv()
-            plane1 = own1 + k1[0] + k1[1] + k1[2]
+            gram_out["321"].wait_recv()
+            plane1 = own1 + k1[0] + k1[1] + k1[2] - times_gram(
+                (z3, g321[:, :RANK]), (y3, g321[:, RANK : 2 * RANK])
+            )
         with jax.named_scope("level2"):
             d2_out.wait_recv()
             z2, _ = solve(2, plane2, m2[...])
-            gram_out["321"].wait_recv()
-            plane1 = plane1 - times_gram(
-                (z3, g321[:, :RANK]), (y3, g321[:, RANK : 2 * RANK]), (z2, g321[:, 2 * RANK :])
-            )
+            plane1 = plane1 - times_gram((z2, g321[:, 2 * RANK :]))
             e1[...] = plane1
             e1_out.start()
         with jax.named_scope("correct_0"):
@@ -483,39 +491,46 @@
             )
             f0[...] = plane0
             f0_out.start()
-            z_out[2].start()
+            z_rest.start()
         with jax.named_scope("level1"):
             e1_out.wait_recv()
-            z1, _ = solve(1, plane1 + l1[0], l1[1] + l1[2])
+            z1, y1 = solve(1, plane1 + l1[0], l1[1] + l1[2])
         with jax.named_scope("correct_by_1"):
             f0_out.wait_recv()
+            near0, far0 = plane0 + l1r[0], l1r[1] + l1r[2]
             gram_out["10"].wait_recv()
-            pair0 = plane0 + l1r[...] - times_gram((z1, g10[...]))
-            e0[...] = pair0
-            e0_out.start()
-            z_out[1].start()
-            for level in (4, 3, 2):
-                z_wait(level, 1)
-            subtract((2, 3, 4), field)
+            half0 = near0 + far0 - times_gram((z1, g10[:, :RANK]), (y1, g10[:, RANK:]))
+            e0[...] = half0
+
+            @pl.when(at_end)
+            def _():
+                e0_out.start()
+
+            z_one.start()
         with jax.named_scope("level0"):
             e0_out.wait_recv()
-            solve(0, pair0 + l0[0], l0[1] + l0[2])
-            z_out[0].start()
+            solve(0, half0, l0[...])
+            z_low.start()
         with jax.named_scope("field_update"):
-            z_wait(1, 1)
-            subtract((1,), field)
-            z_wait(0, 1)
+            z_wait(z_rest, 2, 5, 1)
+            z_wait(z_one, 1, 2, 1)
+            subtract((1, 2, 3, 4), field)
+            z_wait(z_low, 0, 1, 1)
             subtract((0,), out)
         with jax.named_scope("sent"):
             for stage in gram_pair + [
-                p4_out, p3_out, p2_out, p10_out, e3_out, e2_out, h1_out, h0_out, d2_out, e1_out, f0_out, e0_out,
-            ] + z_out:
+                p4_out, p3_out, p2_out, p10_out, e3_out, e2_out, h1_out, h0_out, d2_out, e1_out, f0_out,
+            ] + [z_rest, z_one, z_low]:
                 stage.wait_send()
 
+            @pl.when(at_end)
+            def _():
+                e0_out.wait_send()
+
     assert counter[0] == STAGES
 
 
-STAGES = 40
+STAGES = 39
 
 
 def vmem(*shape, dtype=F32):
@@ -532,20 +547,20 @@
     ]
     scratch += [vmem(RANK, sum(WIDTHS))] * 2
     scratch += [vmem(3, q, width) for width in WIDTHS]
-    scratch += [vmem(q, width * RANK) for width in (1, 1, 1, 1, 2, 1, 3)]
-    scratch += [vmem(3, q, width * RANK) for width in (1, 2, 3)]
-    scratch += [vmem(q, width * RANK) for width in (2, 3, 3, 1, 1, 1)]
-    scratch += [vmem(RANK, width * RANK) for width in (1, 1, 2, 1, 3, 1, 3, 1)]
+    scratch += [vmem(q, width * RANK) for width in (1, 1, 1, 1, 2, 1, 1, 2)]
+    scratch += [vmem(3, q, width * RANK) for width in (1, 2, 1, 2)]
+    scratch += [vmem(q, width * RANK) for width in (2, 3, 3, 1)] + [vmem(3, q, RANK), vmem(q, 2 * RANK)]
+    scratch += [vmem(RANK, width * RANK) for width in (1, 1, 2, 1, 3, 1, 3, 2)]
     scratch += [vmem(CASES, width * RANK) for width in (1, 1, 1, 2)] * 2
     scratch += [vmem(7, q, RANK), vmem(3, q, RANK), vmem(3, q, RANK), vmem(3, q, 2 * RANK)]
     scratch += [vmem(q, RANK), vmem(3, q, RANK)] * 4
     scratch += [vmem(q, RANK), vmem(q, RANK)]
-    scratch += [vmem(q, RANK), vmem(3, q, RANK), vmem(q, RANK), vmem(q, RANK), vmem(q, RANK), vmem(3, q, RANK)]
-    scratch += [vmem(LEVELS, q, RANK), vmem(LEVELS, CASES, RANK)]
+    scratch += [vmem(q, RANK), vmem(3, q, RANK)] * 2 + [vmem(q, RANK), vmem(q, RANK), vmem(2 * q, RANK)]
+    scratch += [vmem(LEVELS, q, RANK), vmem(LEVELS, CASES, RANK), vmem(LEVELS, 7 * q, RANK)]
     scratch += [
         pltpu.SemaphoreType.DMA((LEVELS + 2,)),
         pltpu.SemaphoreType.DMA((rows // ROWS,)),
-        pltpu.SemaphoreType.DMA((STAGES,)),
+        pltpu.SemaphoreType.DMA,
         pltpu.SemaphoreType.DMA((STAGES,)),
     ]
     anywhere = pl.BlockSpec(memory_space=pl.ANY)

time: 40.2 us -> 37.3 us (0.928)
  Pallas kernels: 39.1 us -> 36.2 us
    pallas_call x1, Pallas kernels: 39.1 us -> 36.2 us  [tree_solve(): pl.pallas_call(tree_kernel, out_shape=pltpu.VMEM((rows, CASES), F32), in_...]
where the time goes in v3:
time: 37.3 us; the launch traced here: 37.2 us
  Pallas kernels  36.2 us (97%)
  local copies, waits for them, and re-layouts  0.97 us (3%)
    pallas_call x1, Pallas kernels, tree_solve(): pl.pallas_call(tree_kernel, out_shape=pltpu.VMEM((rows, CASES), F32), in_...  36.2 us
    unnamed x1, local copies, waits for them, and re-layouts  0.97 us

profile of v3, /device:TPU:1, one launch (start us, length us, event | category | flops | bytes accessed | tf_op | source)
XLA Modules:
  0.0 37.2 jit_solution(4878942155501120268)
XLA Ops:
  0.0 36.2 %tree_solve.1 = f32[2048,128]{1,0:T(8,128)S(1)} custom-call(bf16[2048,128]{1,0:T(8,128)(2,1)} %loads_hbm.1, bf16[2048,2048]{1,0:T(8,128)(2,1)} %inverse_hbm.1, bf16[5,2048,128]{2,1,0:T(8,128)(2,1)} %bases_hbm.1, bf16[5,1,256,256]{3,2,1,0:T(8,128)(2,1)} %caps_hbm.1), custom_call_target="tpu_custom_call" | custom-call | tf_op jit(solution)/shard_map/tree_solve/pallas_call | solution.py:567
  36.2 1.0 %copy.6 = f32[2048,128]{1,0:T(8,128)} copy(f32[2048,128]{1,0:T(8,128)S(1)} %tree_solve.1) | data formatting | bytes 2097152

commit v4 on v3

--- a/solution.py
+++ b/solution.py
@@ -53,12 +53,12 @@
 GROUPS = (
     ((4, 3), (1, 0)),
     ((4, 2), (3, 2)),
-    ((4, 1), (3, 1), (2, 1)),
-    ((4, 0), (3, 0), (2, 0)),
+    ((3, 1), (2, 1), (3, 0), (2, 0)),
+    ((4, 1), (4, 0)),
 )
-STARTS = (0, 2 * RANK, 4 * RANK, 7 * RANK)
+STARTS = (0, 2 * RANK, 4 * RANK, 8 * RANK)
 WIDTHS = tuple(len(group) * RANK for group in GROUPS)
-PIECES = ((0, 4 * RANK), (4 * RANK, 7 * RANK), (7 * RANK, 10 * RANK))
+PIECES = ((0, 4 * RANK), (4 * RANK, 8 * RANK), (8 * RANK, 10 * RANK))
 
 
 def tree_kernel(
@@ -75,7 +75,6 @@
     local_sem, chunk_sem, send_sem, recv_sem,
 ):
     rows = field.shape[0]
-    steps = rows // ROWS
     me = lax.axis_index("leaf")
     core = me % 2
     x = (me // 2) % 4
@@ -96,8 +95,10 @@
     loads_copy.start()
     caps_copy = pltpu.make_async_copy(caps_hbm, caps, local_sem.at[LEVELS + 1])
 
+    chunks = ((0, rows // 4), (rows // 4, rows // 4), (rows // 2, rows // 2))
+
     def inverse_copy(step):
-        part = pl.ds(pl.multiple_of(step * ROWS, ROWS), ROWS)
+        part = pl.ds(*chunks[step])
         return pltpu.make_async_copy(inverse_hbm.at[part], inverse.at[part], chunk_sem.at[step])
 
     barrier = pltpu.get_barrier_semaphore()
@@ -128,7 +129,7 @@
     def _():
         greet(chain_partners)
 
-    for step in range(steps):
+    for step in range(len(chunks)):
         inverse_copy(step).start()
     caps_copy.start()
 
@@ -172,8 +173,8 @@
                 device_id=(target,), device_id_type=MESH,
             )
 
-        def start(self):
-            for copy in self.copies:
+        def start(self, which=slice(None)):
+            for copy in self.copies[which]:
                 self.describe(*copy).start()
 
         def wait_recv(self, arrive=None):
@@ -204,8 +205,9 @@
         with jax.named_scope("inverse_in"):
             inverse_copy(step).wait()
         with jax.named_scope("field"):
-            for begin in range(step * ROWS, (step + 1) * ROWS, TILE):
-                part = pl.ds(begin, TILE)
+            begin, size = chunks[step]
+            for at in range(begin, begin + size, TILE):
+                part = pl.ds(at, TILE)
                 field[part, :] = jnp.dot(inverse[part, :], loads[...], preferred_element_type=F32)
 
     field_step(0)
@@ -241,11 +243,8 @@
     def _():
         pair_sum(1)
         gram_rs[2].start()
-        pair_sum(2)
-        gram_rs[3].start()
-
-    for step in range(2, steps):
-        field_step(step)
+
+    field_step(2)
 
     ordered = (p4, p3, p2, p10)
     with jax.named_scope("projections"):
@@ -268,6 +267,8 @@
     @pl.when(core == 0)
     def _():
         proj_pair[2].start()
+        pair_sum(2)
+        gram_rs[3].start()
 
     with jax.named_scope("projections_10"):
         p10[...] = dot_tn(field_b, bcat[:, : 2 * RANK])
@@ -297,8 +298,8 @@
     def subtract(levels, into):
         factors = jnp.concatenate([zbuf[level].astype(BF16) for level in levels], 1)
         low, high = levels[0] * RANK, (levels[-1] + 1) * RANK
-        for step in range(steps):
-            part = pl.ds(step * ROWS, ROWS)
+        for begin in range(0, rows, ROWS):
+            part = pl.ds(begin, ROWS)
             into[part, :] = field[part, :] - dot_nt(bcat[part, low:high], factors)
 
     caps_copy.wait()
@@ -338,15 +339,15 @@
             gram_out["42"].start()
         with jax.named_scope("gram_c"):
             got = row_sum(2)
-            s41_own[...] = got[:, :RANK]
-            s321_own[...] = got[:, RANK:]
+            s321_own[...] = got[:, : 2 * RANK]
+            s320_own[...] = got[:, 2 * RANK :]
             plane_out["321"].start()
-            gram_out["41"].start()
+            plane_out["320"].start()
         with jax.named_scope("gram_d"):
             got = row_sum(3)
-            s40_own[...] = got[:, :RANK]
-            s320_own[...] = got[:, RANK:]
-            plane_out["320"].start()
+            s41_own[...] = got[:, :RANK]
+            s40_own[...] = got[:, RANK:]
+            gram_out["41"].start()
             gram_out["40"].start()
         with jax.named_scope("gram_plane10"):
             plane_out["10"].wait_recv()
@@ -425,6 +426,28 @@
     e1_out = Stage("e1", [(e1, l1.at[j - 1], device(dz=j)) for j in (3, 2, 1)], l1)
     f0_out = Stage("f0", [(f0, l1r.at[j - 1], device(dz=j)) for j in (3, 2, 1)], l1r)
     at_end = (z % 4) * (3 - z % 4) == 0
+    inside = (z % 4) * (3 - z % 4) != 0
+
+    def ends_first(stage):
+        @pl.when(at_end)
+        def _():
+            stage.start(slice(0, 1))
+
+        @pl.when(inside)
+        def _():
+            stage.start(slice(1, 3))
+
+    def the_others(stages):
+        @pl.when(at_end)
+        def _():
+            for stage in stages:
+                stage.start(slice(1, 3))
+
+        @pl.when(inside)
+        def _():
+            for stage in stages:
+                stage.start(slice(0, 1))
+
     e0_out = Stage("e0", [(e0, l0, device(dz=j)) for j in (6, 7)], l0, e0_sent)
 
     @pl.when(core == 1)
@@ -482,7 +505,7 @@
             z2, _ = solve(2, plane2, m2[...])
             plane1 = plane1 - times_gram((z2, g321[:, 2 * RANK :]))
             e1[...] = plane1
-            e1_out.start()
+            ends_first(e1_out)
         with jax.named_scope("correct_0"):
             h0_out.wait_recv()
             gram_out["320"].wait_recv()
@@ -490,7 +513,8 @@
                 (z3, g320[:, :RANK]), (y3, g320[:, RANK : 2 * RANK]), (z2, g320[:, 2 * RANK :])
             )
             f0[...] = plane0
-            f0_out.start()
+            ends_first(f0_out)
+            the_others((e1_out, f0_out))
             z_rest.start()
         with jax.named_scope("level1"):
             e1_out.wait_recv()
@@ -559,7 +583,7 @@
     scratch += [vmem(LEVELS, q, RANK), vmem(LEVELS, CASES, RANK), vmem(LEVELS, 7 * q, RANK)]
     scratch += [
         pltpu.SemaphoreType.DMA((LEVELS + 2,)),
-        pltpu.SemaphoreType.DMA((rows // ROWS,)),
+        pltpu.SemaphoreType.DMA((3,)),
         pltpu.SemaphoreType.DMA,
         pltpu.SemaphoreType.DMA((STAGES,)),
     ]

time: 37.3 us -> 37.1 us (level)
  no operation moved by 1% of the time
where the time goes in v4:
time: 37.1 us; the launch traced here: 37 us
  Pallas kernels  36.1 us (97%)
  local copies, waits for them, and re-layouts  0.97 us (3%)
    pallas_call x1, Pallas kernels, tree_solve(): pl.pallas_call(tree_kernel, out_shape=pltpu.VMEM((rows, CASES), F32), in_...  36.1 us
    unnamed x1, local copies, waits for them, and re-layouts  0.97 us

profile of v4, /device:TPU:1, one launch (start us, length us, event | category | flops | bytes accessed | tf_op | source)
XLA Modules:
  0.0 37.0 jit_solution(10143974525884529923)
XLA Ops:
  0.0 36.1 %tree_solve.1 = f32[2048,128]{1,0:T(8,128)S(1)} custom-call(bf16[2048,128]{1,0:T(8,128)(2,1)} %loads_hbm.1, bf16[2048,2048]{1,0:T(8,128)(2,1)} %inverse_hbm.1, bf16[5,2048,128]{2,1,0:T(8,128)(2,1)} %bases_hbm.1, bf16[5,1,256,256]{3,2,1,0:T(8,128)(2,1)} %caps_hbm.1), custom_call_target="tpu_custom_call" | custom-call | tf_op jit(solution)/shard_map/tree_solve/pallas_call | solution.py:591
  36.1 1.0 %copy.6 = f32[2048,128]{1,0:T(8,128)} copy(f32[2048,128]{1,0:T(8,128)S(1)} %tree_solve.1) | data formatting | bytes 2097152

commit v5 on v4

--- a/solution.py
+++ b/solution.py
@@ -52,23 +52,24 @@
 
 GROUPS = (
     ((4, 3), (1, 0)),
+    ((2, 1), (2, 0)),
     ((4, 2), (3, 2)),
-    ((3, 1), (2, 1), (3, 0), (2, 0)),
+    ((3, 1), (3, 0)),
     ((4, 1), (4, 0)),
 )
-STARTS = (0, 2 * RANK, 4 * RANK, 8 * RANK)
-WIDTHS = tuple(len(group) * RANK for group in GROUPS)
-PIECES = ((0, 4 * RANK), (4 * RANK, 8 * RANK), (8 * RANK, 10 * RANK))
+WIDTH = 2 * RANK
+STARTS = tuple(WIDTH * at for at in range(len(GROUPS)))
+PIECES = ((0, 2 * WIDTH), (2 * WIDTH, 4 * WIDTH), (4 * WIDTH, 5 * WIDTH))
 
 
 def tree_kernel(
     loads_hbm, inverse_hbm, bases_hbm, caps_hbm,
     out,
     loads, inverse, bcat, caps, field,
-    gram, gram_in, sa_rs, sb_rs, sc_rs, sd_rs,
-    s43_own, s42_own, s32_own, s41_own, s321_own, s40_own, s10_own, s320_own, s32_y, s321_y, s10_y, s320_y,
-    t32_own, t321_own, t320_own, t10_own, t10_z, u10_own,
-    g43, g42, g32, g41, g321, g40, g320, g10,
+    gram, gram_in, s0_rs, s1_rs, s2_rs, s3_rs, s4_rs,
+    s43_own, s10_own, s42_own, s32_own, s31_own, s30_own, s41_own, s40_own, s32_y, s31_y, s30_y, s10_y,
+    plane_own, plane_x, t32_own, t31_own, t30_own, t2_own, t10_own, t10_z, u10_own,
+    g43, g42, g32, g41, g31, g40, g30, g2, g10,
     p4, p3, p2, p10, p4_in, p3_in, p2_in, p10_in, p4_rs, p3_rs, p2_rs, p10_rs,
     e3, l3, e2, l2, h1, k1, h0, k0, d2, m2, e1, l1, f0, l1r, e0, l0, e0_sent,
     zown, zbuf, z_sent,
@@ -112,9 +113,11 @@
         + [device(dy=j, on=0) for j in (1, 2, 3)]
         + [device(dz=j, on=0) for j in (1, 2, 3)]
         + [device(dx=j, on=1) for j in range(4)]
+        + [device(dy=j, on=1) for j in (1, 2, 3)]
     )
     chain_partners = (
         [device(dx=j, on=0) for j in range(4)]
+        + [device(dy=j, on=0) for j in (1, 2, 3)]
         + [device(dx=j) for j in (1, 2, 3)]
         + [device(dx=j, dy=1) for j in range(4)]
         + [device(dy=j) for j in (2, 3)]
@@ -212,18 +215,23 @@
 
     field_step(0)
 
-    rs_slots = (sa_rs, sb_rs, sc_rs, sd_rs)
-    gram_rs = [
-        Stage(
-            "gram_row",
-            [
-                (gram.at[quarter(flips(x, j)), pl.ds(begin, width)], slots.at[j - 1], device(dx=j, on=0))
+    rs_slots = (s0_rs, s1_rs, s2_rs, s3_rs, s4_rs)
+
+    def deal(group):
+        columns, slots = pl.ds(STARTS[group], WIDTH), rs_slots[group]
+        if group == 1:
+            copies = [
+                (gram.at[quarter(flips(y, j)), columns], slots.at[j - 1], device(dy=j, on=0))
                 for j in (2, 3, 1)
-            ],
-            slots,
-        )
-        for begin, width, slots in zip(STARTS, WIDTHS, rs_slots)
-    ]
+            ]
+        else:
+            copies = [
+                (gram.at[quarter(flips(x, j)), columns], slots.at[j - 1], device(dx=j, on=0))
+                for j in (2, 3, 1)
+            ]
+        return Stage("gram_row%d" % group, copies, slots)
+
+    gram_rs = [deal(group) for group in range(len(GROUPS))]
 
     def pair_sum(piece):
         with jax.named_scope("pair_sums"):
@@ -243,6 +251,7 @@
     def _():
         pair_sum(1)
         gram_rs[2].start()
+        gram_rs[3].start()
 
     field_step(2)
 
@@ -268,7 +277,7 @@
     def _():
         proj_pair[2].start()
         pair_sum(2)
-        gram_rs[3].start()
+        gram_rs[4].start()
 
     with jax.named_scope("projections_10"):
         p10[...] = dot_tn(field_b, bcat[:, : 2 * RANK])
@@ -304,76 +313,76 @@
 
     caps_copy.wait()
 
+    own_y = quarter(y)
     gram_out = {
         name: Stage("gram_" + name, [(src, dst.at[own_q], device(dx=j)) for j in (2, 3, 1, 0)], dst)
         for name, src, dst in (
             ("43", s43_own, g43), ("42", s42_own, g42), ("32", t32_own, g32), ("41", s41_own, g41),
-            ("321", t321_own, g321), ("40", s40_own, g40), ("320", t320_own, g320), ("10", u10_own, g10),
+            ("31", t31_own, g31), ("40", s40_own, g40), ("30", t30_own, g30), ("10", u10_own, g10),
         )
     }
-    plane_out = {
-        name: Stage("plane" + name, [(src, dst.at[j - 1], device(dy=j, on=0)) for j in (1, 2, 3)], dst)
-        for name, src, dst in (("32", s32_own, s32_y), ("321", s321_own, s321_y), ("10", s10_own, s10_y), ("320", s320_own, s320_y))
+    gram_out["2"] = Stage("gram_2", [(t2_own, g2.at[own_y], device(dy=j)) for j in (2, 3, 1, 0)], g2)
+    column_out = {
+        name: Stage("column" + name, [(src, dst.at[j - 1], device(dy=j, on=0)) for j in (2, 3, 1)], dst)
+        for name, src, dst in (
+            ("32", s32_own, s32_y), ("31", s31_own, s31_y), ("30", s30_own, s30_y), ("10", s10_own, s10_y),
+        )
     }
+    plane_out = Stage(
+        "plane", [(plane_own, plane_x.at[j - 1], device(dx=j, on=0)) for j in (2, 3, 1)], plane_x
+    )
     pair_out = Stage("pair", [(t10_own, t10_z.at[j - 1], device(dz=j, on=0)) for j in (3, 2, 1)], t10_z)
 
-    def row_sum(group):
+    def dealt(group, rows_own):
         gram_rs[group].wait_recv()
         slots = rs_slots[group]
-        begin, width = STARTS[group], WIDTHS[group]
-        return gram[own_q, begin : begin + width] + slots[0] + slots[1] + slots[2]
-
-    @pl.when(core == 0)
-    def _():
-        with jax.named_scope("gram_a"):
-            got = row_sum(0)
+        begin = STARTS[group]
+        return gram[rows_own, begin : begin + WIDTH] + slots[0] + slots[1] + slots[2]
+
+    def child_sums(name, own, slots, both):
+        column_out[name].wait_recv()
+        both[:, :RANK] = own[...] + slots[0]
+        both[:, RANK:] = slots[1] + slots[2]
+        gram_out[name].start()
+
+    @pl.when(core == 0)
+    def _():
+        with jax.named_scope("gram_rows"):
+            got = dealt(0, own_q)
             s43_own[...] = got[:, :RANK]
             s10_own[...] = got[:, RANK:]
             gram_out["43"].start()
-            plane_out["10"].start()
-        with jax.named_scope("gram_b"):
-            got = row_sum(1)
+            column_out["10"].start()
+            got = dealt(2, own_q)
             s42_own[...] = got[:, :RANK]
             s32_own[...] = got[:, RANK:]
-            plane_out["32"].start()
+            column_out["32"].start()
             gram_out["42"].start()
-        with jax.named_scope("gram_c"):
-            got = row_sum(2)
-            s321_own[...] = got[:, : 2 * RANK]
-            s320_own[...] = got[:, 2 * RANK :]
-            plane_out["321"].start()
-            plane_out["320"].start()
-        with jax.named_scope("gram_d"):
-            got = row_sum(3)
+            plane_own[...] = dealt(1, own_y)
+            plane_out.start()
+            got = dealt(3, own_q)
+            s31_own[...] = got[:, :RANK]
+            s30_own[...] = got[:, RANK:]
+            column_out["31"].start()
+            column_out["30"].start()
+            got = dealt(4, own_q)
             s41_own[...] = got[:, :RANK]
             s40_own[...] = got[:, RANK:]
             gram_out["41"].start()
             gram_out["40"].start()
         with jax.named_scope("gram_plane10"):
-            plane_out["10"].wait_recv()
+            column_out["10"].wait_recv()
             t10_own[...] = s10_own[...] + s10_y[0] + s10_y[1] + s10_y[2]
             pair_out.start()
-        with jax.named_scope("gram_plane32"):
-            plane_out["32"].wait_recv()
-            t32_own[:, :RANK] = s32_own[...] + s32_y[0]
-            t32_own[:, RANK:] = s32_y[1] + s32_y[2]
-            gram_out["32"].start()
-        with jax.named_scope("gram_plane321"):
-            plane_out["321"].wait_recv()
-            near = s321_own[...] + s321_y[0]
-            far = s321_y[1] + s321_y[2]
-            t321_own[:, :RANK] = near[:, :RANK]
-            t321_own[:, RANK : 2 * RANK] = far[:, :RANK]
-            t321_own[:, 2 * RANK :] = near[:, RANK:] + far[:, RANK:]
-            gram_out["321"].start()
-        with jax.named_scope("gram_plane320"):
-            plane_out["320"].wait_recv()
-            near = s320_own[...] + s320_y[0]
-            far = s320_y[1] + s320_y[2]
-            t320_own[:, :RANK] = near[:, :RANK]
-            t320_own[:, RANK : 2 * RANK] = far[:, :RANK]
-            t320_own[:, 2 * RANK :] = near[:, RANK:] + far[:, RANK:]
-            gram_out["320"].start()
+        with jax.named_scope("gram_children"):
+            child_sums("32", s32_own, s32_y, t32_own)
+            child_sums("31", s31_own, s31_y, t31_own)
+        with jax.named_scope("gram_plane_sum"):
+            plane_out.wait_recv()
+            t2_own[...] = plane_own[...] + plane_x[0] + plane_x[1] + plane_x[2]
+            gram_out["2"].start()
+        with jax.named_scope("gram_children"):
+            child_sums("30", s30_own, s30_y, t30_own)
         with jax.named_scope("gram_pair"):
             pair_out.wait_recv()
             u10_own[:, :RANK] = t10_own[...] + t10_z[0]
@@ -387,7 +396,11 @@
             subtract((0,), out)
         with jax.named_scope("sent"):
             for stage in (
-                gram_rs + list(gram_out.values()) + list(plane_out.values()) + [pair_out] + proj_pair
+                gram_rs
+                + list(gram_out.values())
+                + list(column_out.values())
+                + [plane_out, pair_out]
+                + proj_pair
             ):
                 stage.wait_send()
 
@@ -496,21 +509,22 @@
             d2[...] = plane2
             d2_out.start()
             h1_out.wait_recv()
-            gram_out["321"].wait_recv()
+            gram_out["31"].wait_recv()
             plane1 = own1 + k1[0] + k1[1] + k1[2] - times_gram(
-                (z3, g321[:, :RANK]), (y3, g321[:, RANK : 2 * RANK])
+                (z3, g31[:, :RANK]), (y3, g31[:, RANK:])
             )
         with jax.named_scope("level2"):
             d2_out.wait_recv()
             z2, _ = solve(2, plane2, m2[...])
-            plane1 = plane1 - times_gram((z2, g321[:, 2 * RANK :]))
+            gram_out["2"].wait_recv()
+            plane1 = plane1 - times_gram((z2, g2[:, :RANK]))
             e1[...] = plane1
             ends_first(e1_out)
         with jax.named_scope("correct_0"):
             h0_out.wait_recv()
-            gram_out["320"].wait_recv()
+            gram_out["30"].wait_recv()
             plane0 = own0 + k0[0] + k0[1] + k0[2] - times_gram(
-                (z3, g320[:, :RANK]), (y3, g320[:, RANK : 2 * RANK]), (z2, g320[:, 2 * RANK :])
+                (z3, g30[:, :RANK]), (y3, g30[:, RANK:]), (z2, g2[:, RANK:])
             )
             f0[...] = plane0
             ends_first(f0_out)
@@ -554,7 +568,7 @@
     assert counter[0] == STAGES
 
 
-STAGES = 39
+STAGES = 42
 
 
 def vmem(*shape, dtype=F32):
@@ -569,12 +583,12 @@
         vmem(rows, LEVELS * RANK, dtype=BF16), vmem(*caps.shape, dtype=BF16),
         vmem(rows, CASES),
     ]
-    scratch += [vmem(RANK, sum(WIDTHS))] * 2
-    scratch += [vmem(3, q, width) for width in WIDTHS]
-    scratch += [vmem(q, width * RANK) for width in (1, 1, 1, 1, 2, 1, 1, 2)]
-    scratch += [vmem(3, q, width * RANK) for width in (1, 2, 1, 2)]
-    scratch += [vmem(q, width * RANK) for width in (2, 3, 3, 1)] + [vmem(3, q, RANK), vmem(q, 2 * RANK)]
-    scratch += [vmem(RANK, width * RANK) for width in (1, 1, 2, 1, 3, 1, 3, 2)]
+    scratch += [vmem(RANK, WIDTH * len(GROUPS))] * 2
+    scratch += [vmem(3, q, WIDTH)] * len(GROUPS)
+    scratch += [vmem(q, RANK)] * 8 + [vmem(3, q, RANK)] * 4
+    scratch += [vmem(q, WIDTH), vmem(3, q, WIDTH)] + [vmem(q, WIDTH)] * 4
+    scratch += [vmem(q, RANK), vmem(3, q, RANK), vmem(q, WIDTH)]
+    scratch += [vmem(RANK, width * RANK) for width in (1, 1, 2, 1, 2, 1, 2, 2, 2)]
     scratch += [vmem(CASES, width * RANK) for width in (1, 1, 1, 2)] * 2
     scratch += [vmem(7, q, RANK), vmem(3, q, RANK), vmem(3, q, RANK), vmem(3, q, 2 * RANK)]
     scratch += [vmem(q, RANK), vmem(3, q, RANK)] * 4

time: 37.1 us -> 36.7 us (0.989)
  Pallas kernels: 36.1 us -> 35.6 us
    pallas_call x1, Pallas kernels: 36.1 us -> 35.6 us  [tree_solve(): pl.pallas_call(tree_kernel, out_shape=pltpu.VMEM((rows, CASES), F32), in_...]
where the time goes in v5:
time: 36.7 us; the launch traced here: 36.6 us
  Pallas kernels  35.6 us (97%)
  local copies, waits for them, and re-layouts  0.97 us (3%)
    pallas_call x1, Pallas kernels, tree_solve(): pl.pallas_call(tree_kernel, out_shape=pltpu.VMEM((rows, CASES), F32), in_...  35.6 us
    unnamed x1, local copies, waits for them, and re-layouts  0.97 us

profile of v5, /device:TPU:1, one launch (start us, length us, event | category | flops | bytes accessed | tf_op | source)
XLA Modules:
  0.0 36.6 jit_solution(3243929496418071132)
XLA Ops:
  0.0 35.6 %tree_solve.1 = f32[2048,128]{1,0:T(8,128)S(1)} custom-call(bf16[2048,128]{1,0:T(8,128)(2,1)} %loads_hbm.1, bf16[2048,2048]{1,0:T(8,128)(2,1)} %inverse_hbm.1, bf16[5,2048,128]{2,1,0:T(8,128)(2,1)} %bases_hbm.1, bf16[5,1,256,256]{3,2,1,0:T(8,128)(2,1)} %caps_hbm.1), custom_call_target="tpu_custom_call" | custom-call | tf_op jit(solution)/shard_map/tree_solve/pallas_call | solution.py:605
  35.7 1.0 %copy.6 = f32[2048,128]{1,0:T(8,128)} copy(f32[2048,128]{1,0:T(8,128)S(1)} %tree_solve.1) | data formatting | bytes 2097152

commit v6 on v5

--- a/solution.py
+++ b/solution.py
@@ -158,13 +158,13 @@
         with jax.named_scope("meet"):
             pl.semaphore_wait(barrier, len(chain_partners))
 
-    counter = [0]
+    counter = {"both": 0, "core0": 3, "core1": 3}
 
     class Stage:
-        def __init__(self, name, copies, arrive, leave=None):
+        def __init__(self, name, copies, arrive, leave=None, heard="core1"):
             self.name = name
-            self.number = counter[0]
-            counter[0] += 1
+            self.number = counter[heard]
+            counter[heard] += 1
             self.copies = copies
             self.arrive = arrive
             self.leave = arrive if leave is None else leave
@@ -193,7 +193,7 @@
 
     other = device(on=1 - core)
     gram_pair = [
-        Stage("gram_in", [(gram.at[:, low:high], gram_in.at[:, low:high], other)], gram_in.at[:, low:high])
+        Stage("gram_in", [(gram.at[:, low:high], gram_in.at[:, low:high], other)], gram_in.at[:, low:high], heard="core0")
         for low, high in PIECES
     ]
 
@@ -229,7 +229,7 @@
                 (gram.at[quarter(flips(x, j)), columns], slots.at[j - 1], device(dx=j, on=0))
                 for j in (2, 3, 1)
             ]
-        return Stage("gram_row%d" % group, copies, slots)
+        return Stage("gram_row%d" % group, copies, slots, heard="core0")
 
     gram_rs = [deal(group) for group in range(len(GROUPS))]
 
@@ -296,7 +296,7 @@
                 (zown.at[levels], zbuf.at[levels, own_q], device(dx=j, on=on))
                 for j, on in z_targets
             ],
-            zbuf.at[levels], z_sent.at[levels],
+            zbuf.at[levels], z_sent.at[levels], heard="both",
         )
 
     z_low, z_one, z_rest = z_stage(0, 1), z_stage(1, 2), z_stage(2, 5)
@@ -323,15 +323,17 @@
     }
     gram_out["2"] = Stage("gram_2", [(t2_own, g2.at[own_y], device(dy=j)) for j in (2, 3, 1, 0)], g2)
     column_out = {
-        name: Stage("column" + name, [(src, dst.at[j - 1], device(dy=j, on=0)) for j in (2, 3, 1)], dst)
+        name: Stage(
+            "column" + name, [(src, dst.at[j - 1], device(dy=j, on=0)) for j in (2, 3, 1)], dst, heard="core0"
+        )
         for name, src, dst in (
             ("32", s32_own, s32_y), ("31", s31_own, s31_y), ("30", s30_own, s30_y), ("10", s10_own, s10_y),
         )
     }
     plane_out = Stage(
-        "plane", [(plane_own, plane_x.at[j - 1], device(dx=j, on=0)) for j in (2, 3, 1)], plane_x
+        "plane", [(plane_own, plane_x.at[j - 1], device(dx=j, on=0)) for j in (2, 3, 1)], plane_x, heard="core0"
     )
-    pair_out = Stage("pair", [(t10_own, t10_z.at[j - 1], device(dz=j, on=0)) for j in (3, 2, 1)], t10_z)
+    pair_out = Stage("pair", [(t10_own, t10_z.at[j - 1], device(dz=j, on=0)) for j in (3, 2, 1)], t10_z, heard="core0")
 
     def dealt(group, rows_own):
         gram_rs[group].wait_recv()
@@ -565,10 +567,10 @@
             def _():
                 e0_out.wait_send()
 
-    assert counter[0] == STAGES
-
-
-STAGES = 42
+    assert max(counter.values()) == STAGES and counter["both"] == 3
+
+
+STAGES = 28
 
 
 def vmem(*shape, dtype=F32):

time: 36.7 us -> 36.6 us (level)
  no operation moved by 1% of the time
where the time goes in v6:
time: 36.6 us; the launch traced here: 36.5 us
  Pallas kernels  35.5 us (97%)
  local copies, waits for them, and re-layouts  0.97 us (3%)
    pallas_call x1, Pallas kernels, tree_solve(): pl.pallas_call(tree_kernel, out_shape=pltpu.VMEM((rows, CASES), F32), in_...  35.5 us
    unnamed x1, local copies, waits for them, and re-layouts  0.97 us

profile of v6, /device:TPU:1, one launch (start us, length us, event | category | flops | bytes accessed | tf_op | source)
XLA Modules:
  0.0 36.5 jit_solution(17275949055709901747)
XLA Ops:
  0.0 35.5 %tree_solve.1 = f32[2048,128]{1,0:T(8,128)S(1)} custom-call(bf16[2048,128]{1,0:T(8,128)(2,1)} %loads_hbm.1, bf16[2048,2048]{1,0:T(8,128)(2,1)} %inverse_hbm.1, bf16[5,2048,128]{2,1,0:T(8,128)(2,1)} %bases_hbm.1, bf16[5,1,256,256]{3,2,1,0:T(8,128)(2,1)} %caps_hbm.1), custom_call_target="tpu_custom_call" | custom-call | tf_op jit(solution)/shard_map/tree_solve/pallas_call | solution.py:607
  35.5 1.0 %copy.6 = f32[2048,128]{1,0:T(8,128)} copy(f32[2048,128]{1,0:T(8,128)S(1)} %tree_solve.1) | data formatting | bytes 2097152

commit v7 on v6

--- a/solution.py
+++ b/solution.py
@@ -258,9 +258,10 @@
     ordered = (p4, p3, p2, p10)
     with jax.named_scope("projections"):
         field_b = field[...].astype(BF16)
-        got = dot_tn(field_b, bcat[:, 3 * RANK :])
-        p4[...] = got[:, RANK:]
-        p3[...] = got[:, :RANK]
+        got = dot_tn(field_b, bcat[:, 2 * RANK :])
+        p4[...] = got[:, 2 * RANK :]
+        p3[...] = got[:, RANK : 2 * RANK]
+        p2[...] = got[:, :RANK]
     ordered_in = (p4_in, p3_in, p2_in, p10_in)
     proj_pair = [Stage("proj_in", [(src, dst, other)], dst) for src, dst in zip(ordered, ordered_in)]
     own_q = quarter(x)
@@ -269,9 +270,6 @@
     def _():
         proj_pair[0].start()
         proj_pair[1].start()
-
-    with jax.named_scope("projection_2"):
-        p2[...] = dot_tn(field_b, bcat[:, 2 * RANK : 3 * RANK])
 
     @pl.when(core == 0)
     def _():

time: 36.6 us -> 36.3 us (level)
  no operation moved by 1% of the time
where the time goes in v7:
time: 36.3 us
  Pallas kernels  35.3 us (97%)
  local copies, waits for them, and re-layouts  0.97 us (3%)
    pallas_call x1, Pallas kernels, tree_solve(): pl.pallas_call(tree_kernel, out_shape=pltpu.VMEM((rows, CASES), F32), in_...  35.3 us
    unnamed x1, local copies, waits for them, and re-layouts  0.97 us

profile of v7, /device:TPU:1, one launch (start us, length us, event | category | flops | bytes accessed | tf_op | source)
XLA Modules:
  0.0 36.3 jit_solution(1725666333001854183)
XLA Ops:
  0.0 35.3 %tree_solve.1 = f32[2048,128]{1,0:T(8,128)S(1)} custom-call(bf16[2048,128]{1,0:T(8,128)(2,1)} %loads_hbm.1, bf16[2048,2048]{1,0:T(8,128)(2,1)} %inverse_hbm.1, bf16[5,2048,128]{2,1,0:T(8,128)(2,1)} %bases_hbm.1, bf16[5,1,256,256]{3,2,1,0:T(8,128)(2,1)} %caps_hbm.1), custom_call_target="tpu_custom_call" | custom-call | tf_op jit(solution)/shard_map/tree_solve/pallas_call | solution.py:605
  35.3 1.0 %copy.6 = f32[2048,128]{1,0:T(8,128)} copy(f32[2048,128]{1,0:T(8,128)S(1)} %tree_solve.1) | data formatting | bytes 2097152
